TPU v7x, 512 devices: a whole 4x4x16 slice. The times are simulated.
512 devices in a mesh: seq: 32 (over z_hi, x, core), dp: 16 (over y, z_lo).
Axes of the slice: x: 4, y: 4, z: 16 (z_hi: 4, z_lo: 4; z = z_hi * 4 + z_lo), core: 2. Of those that a mesh axis runs over, the one named last changes fastest.
Arguments:
- queries: bfloat16 [16384, 2048], P('seq', 'dp'), may hold values from -6 to 6
- keys: bfloat16 [16384, 2048], P('seq', 'dp'), may hold values from -6 to 6
- values: bfloat16 [16384, 2048], P('seq', 'dp'), may hold values from -6 to 6
- out_weight: bfloat16 [2048, 2048], P('seq', 'dp'), may hold values from -2 to 2
- grad_out: bfloat16 [16384, 2048], P('seq', 'dp'), may hold values from -1.5 to 1.5
- pattern: int32 [16, 256, 5], replicated, may hold values from 0 to 255, as said below
Outputs:
- output: bfloat16 [16384, 2048], P('seq', 'dp')
- grad_queries: bfloat16 [16384, 2048], P('seq', 'dp')
- grad_keys: bfloat16 [16384, 2048], P('seq', 'dp')
- grad_values: bfloat16 [16384, 2048], P('seq', 'dp')
Inputs may be any that keep to these rules, and one draw needn't show every extreme that they name: pattern[h, b, 0] and pattern[h, b, 1] are the two global key blocks of head h, equal for every b. For each head h and each s, the random entries pattern[h, b, 2:] over the query blocks b = s * 8 to (s + 1) * 8 - 1 name at most 2 blocks in any aligned range of 8 blocks (counting repeats), and exactly 2 in one such range. Entries may repeat one another or a local block.
All inputs are finite; a program needn't handle non-finite values.
Results may differ from a plain program's by a relative error of at most 0.039.
Values may be sent and summed in bfloat16 or wider, within the bound.
A program may use at most 64 MiB of HBM per device.

v0:
```python
import jax
import jax.numpy as jnp
from jax import lax
from jax.sharding import PartitionSpec as P

HEAD_DIM = 128
BLOCK = 64


def with_halo(cells, sides, width):
    for axis, dim in sides:
        count = lax.axis_size(axis)
        head = lax.slice_in_dim(cells, 0, width, axis=dim)
        tail = lax.slice_in_dim(cells, cells.shape[dim] - width, cells.shape[dim], axis=dim)
        cells = jnp.concatenate(
            [
                lax.ppermute(tail, axis, [(i, (i + 1) % count) for i in range(count)]),
                cells,
                lax.ppermute(head, axis, [((i + 1) % count, i) for i in range(count)]),
            ],
            axis=dim,
        )
    return cells


def owner_ranks(random_blocks, block_span):
    owners = random_blocks // block_span
    count = random_blocks.shape[-1]
    same_owner = owners[..., :, None] == owners[..., None, :]
    order = jnp.arange(count, dtype=jnp.int32)
    earlier = order[None, :] < order[:, None]
    ranks = jnp.sum((same_owner & earlier).astype(jnp.int32), axis=-1)
    return (owners, ranks)


def per_device(queries, keys, values, out_weight, grad_out, pattern):
    seq_count = lax.axis_size("seq")
    seq_pos = lax.axis_index("seq")
    data_pos = lax.axis_index("dp")
    tokens, width = queries.shape
    heads_here = width // HEAD_DIM
    q_blocks = tokens // BLOCK
    random_count = pattern.shape[2] - 2
    entries = q_blocks * random_count
    capacity = max(2, 3 * entries // (2 * seq_count))
    attention_scaling = HEAD_DIM ** (-0.5)
    highest = lax.Precision.HIGHEST
    f32 = jnp.float32
    bf16 = jnp.bfloat16
    weight_cols = lax.all_gather(out_weight, "seq", axis=0, tiled=True)
    weight_rows = lax.all_to_all(weight_cols, "dp", split_axis=0, concat_axis=1, tiled=True)
    head_pattern = lax.dynamic_slice_in_dim(pattern, data_pos * heads_here, heads_here, 0)
    global_list = head_pattern[:, 0, 0:2]
    all_random = head_pattern[:, :, 2:].reshape(heads_here, seq_count, entries)
    my_random = lax.dynamic_slice_in_dim(all_random, seq_pos, 1, 1)[:, 0]
    my_owner, my_rank = owner_ranks(my_random, q_blocks)
    all_owner, all_rank = owner_ranks(all_random, q_blocks)
    seq_ids = jnp.arange(seq_count, dtype=jnp.int32)
    slot_ids = jnp.arange(capacity, dtype=jnp.int32)
    block_ids = jnp.arange(q_blocks, dtype=jnp.int32)
    slot_place = (
        (my_owner[:, None, None, :] == seq_ids[None, :, None, None])
        & (my_rank[:, None, None, :] == slot_ids[None, None, :, None])
    ).astype(f32)
    sender_slots = (all_owner[:, :, None, :] == seq_pos) & (
        all_rank[:, :, None, :] == slot_ids[None, None, :, None]
    )
    local_block = all_random - seq_pos * q_blocks
    sender_hits = sender_slots[..., None] & (local_block[:, :, None, :, None] == block_ids)
    slot_pick = jnp.sum(sender_hits.astype(f32), axis=3)
    global_hit = (global_list[:, :, None] - seq_pos * q_blocks == block_ids).astype(f32)

    def to_blocks(rows):
        return rows.reshape(q_blocks, BLOCK, heads_here, HEAD_DIM).transpose(2, 0, 1, 3)

    def to_rows(blocks):
        return blocks.transpose(1, 2, 0, 3).reshape(tokens, width)

    query_block_list = to_blocks(queries)
    pair_blocks = jnp.stack([to_blocks(keys), to_blocks(values)])
    edge_rows = with_halo(jnp.stack([keys, values]), (("seq", 1),), BLOCK)
    edge_blocks = edge_rows.reshape(2, q_blocks + 2, BLOCK, heads_here, HEAD_DIM).transpose(
        0, 3, 1, 2, 4
    )
    window = jnp.stack(
        [
            edge_blocks[:, :, 0:q_blocks],
            edge_blocks[:, :, 1 : q_blocks + 1],
            edge_blocks[:, :, 2 : q_blocks + 2],
        ],
        axis=3,
    )
    global_part = jnp.einsum(
        "hjq,shqxy->shjxy", global_hit.astype(bf16), pair_blocks, preferred_element_type=f32
    )
    global_pair = lax.psum(global_part.astype(jnp.bfloat16), "seq").astype(jnp.float32).astype(bf16)
    global_tiles = jnp.broadcast_to(
        global_pair[:, :, None], (2, heads_here, q_blocks, 2, BLOCK, HEAD_DIM)
    )
    outbound = jnp.einsum(
        "hrcq,shqxy->shrcxy", slot_pick.astype(bf16), pair_blocks, preferred_element_type=f32
    ).astype(bf16)
    arrived = lax.all_to_all(outbound, "seq", split_axis=2, concat_axis=2, tiled=True)
    random_tiles = jnp.einsum(
        "hoce,shocxy->shexy", slot_place.astype(bf16), arrived, preferred_element_type=f32
    ).astype(bf16)
    random_tiles = random_tiles.reshape(2, heads_here, q_blocks, random_count, BLOCK, HEAD_DIM)
    listed = jnp.concatenate([window, global_tiles, random_tiles], axis=3)
    listed = listed.reshape(2, heads_here, q_blocks, -1, HEAD_DIM)
    key_block_tiles = listed[0]
    value_block_tiles = listed[1]
    logit_scores = (
        jnp.einsum("hbqe,hbke->hbqk", query_block_list, key_block_tiles, preferred_element_type=f32)
        * attention_scaling
    )
    maxima = jnp.max(logit_scores, axis=-1, keepdims=True)
    exp_scores = jnp.exp(logit_scores - maxima)
    totals = jnp.sum(exp_scores, axis=-1, keepdims=True)
    probs_full = exp_scores / totals
    probabilities_reduced = probs_full.astype(bf16)
    context_output = jnp.einsum(
        "hbqk,hbke->hbqe", probabilities_reduced, value_block_tiles, preferred_element_type=f32
    ).astype(bf16)
    context_rows = to_rows(context_output)
    weight_part = weight_cols
    output = jnp.dot(
        lax.all_gather(context_rows, "dp", axis=1, tiled=True),
        weight_part,
        preferred_element_type=f32,
    ).astype(bf16)
    weight_part = weight_rows
    grad_context = lax.dot_general(
        lax.all_gather(grad_out, "dp", axis=1, tiled=True),
        weight_part,
        (((1,), (1,)), ((), ())),
        preferred_element_type=f32,
    ).astype(bf16)
    gradient_blockwise = to_blocks(grad_context)
    delta_sum = jnp.sum(
        gradient_blockwise.astype(f32) * context_output.astype(f32), axis=-1, keepdims=True
    )
    gradient_probabilities = jnp.einsum(
        "hbqe,hbke->hbqk", gradient_blockwise, value_block_tiles, preferred_element_type=f32
    )
    score_gradient = (probs_full * (gradient_probabilities - delta_sum)).astype(bf16)
    query_gradient = (
        jnp.einsum("hbqk,hbke->hbqe", score_gradient, key_block_tiles, preferred_element_type=f32)
        * attention_scaling
    ).astype(bf16)
    near_cols = 5 * BLOCK
    near_keys = (
        jnp.einsum(
            "hbqk,hbqe->hbke",
            score_gradient[..., :near_cols],
            query_block_list,
            preferred_element_type=f32,
        )
        * attention_scaling
    )
    near_values = jnp.einsum(
        "hbqk,hbqe->hbke",
        probabilities_reduced[..., :near_cols],
        gradient_blockwise,
        preferred_element_type=f32,
    )
    near_terms = jnp.stack([near_keys, near_values]).reshape(
        2, heads_here, q_blocks, 5, BLOCK, HEAD_DIM
    )

    def padding(before, after):
        return ((0, 0), (0, 0), (before, after), (0, 0), (0, 0))

    spread_terms = (
        jnp.pad(near_terms[:, :, :, 0], padding(0, 2))
        + jnp.pad(near_terms[:, :, :, 1], padding(1, 1))
        + jnp.pad(near_terms[:, :, :, 2], padding(2, 0))
    )
    own_grads = spread_terms[:, :, 1 : q_blocks + 1]
    rim_terms = jnp.concatenate(
        [spread_terms[:, :, 0:1], spread_terms[:, :, q_blocks + 1 :]], axis=2
    )
    rim_terms = with_halo(rim_terms.astype(jnp.bfloat16), (("seq", 2),), 1).astype(rim_terms.dtype)
    own_grads = own_grads.at[:, :, 0].add(rim_terms[:, :, 0])
    own_grads = own_grads.at[:, :, q_blocks - 1].add(rim_terms[:, :, 3])
    global_terms = lax.psum(
        jnp.sum(near_terms[:, :, :, 3:5], axis=2).astype(jnp.bfloat16), "seq"
    ).astype(jnp.float32)
    own_grads = own_grads + jnp.einsum(
        "hjq,shjxy->shqxy", global_hit, global_terms, precision=highest
    )
    far_keys = (
        jnp.einsum(
            "hbqk,hbqe->hbke",
            score_gradient[..., near_cols:],
            query_block_list,
            preferred_element_type=f32,
        )
        * attention_scaling
    )
    far_values = jnp.einsum(
        "hbqk,hbqe->hbke",
        probabilities_reduced[..., near_cols:],
        gradient_blockwise,
        preferred_element_type=f32,
    )
    far_terms = jnp.stack([far_keys, far_values]).reshape(2, heads_here, entries, BLOCK, HEAD_DIM)
    outgoing = jnp.einsum("hoce,shexy->shocxy", slot_place, far_terms, precision=highest)
    slot_terms = lax.all_to_all(
        outgoing.astype(jnp.bfloat16), "seq", split_axis=2, concat_axis=2, tiled=True
    ).astype(outgoing.dtype)
    own_grads = own_grads + jnp.einsum(
        "hrcq,shrcxy->shqxy", slot_pick, slot_terms, precision=highest
    )
    final_grads = own_grads.astype(bf16)
    return (output, to_rows(query_gradient), to_rows(final_grads[0]), to_rows(final_grads[1]))


def solution(mesh):
    placed = (P("seq", "dp"), P("seq", "dp"), P("seq", "dp"), P("seq", "dp"), P("seq", "dp"), P())
    return jax.shard_map(
        per_device,
        mesh=mesh,
        in_specs=placed,
        out_specs=(P("seq", "dp"), P("seq", "dp"), P("seq", "dp"), P("seq", "dp")),
        check_vma=False,
    )
```

profile of v0, /device:TPU:7, one launch (start us, length us, event | category | flops | bytes accessed | tf_op | source)
XLA Modules:
  0.0 916.9 jit_solution(2702947916150896872)
XLA Ops:
  8.0 52.4 %all_gather.10 = bf16[2048,128]{1,0:T(8,128)(2,1)} all-gather(bf16[64,128]{1,0:T(8,128)(2,1)} %param.13), channel_id=1, replica_groups=mesh['seq'=32,'dp'=16] {'seq'}, dimensions={0}, use_global_device_ids=true | all-gather | bytes 540672 | tf_op jit(solution)/shard_map/all_gather | solution.py:50
  60.4 8.6 all-to-all-start.1
  69.0 0.8 constant_dynamic-slice_fusion.1
  70.7 0.7 convert_bitcast_fusion.1
  71.5 3.7 copy.117
  75.1 9.8 %all-to-all-done.1 = bf16[16,128,128]{2,1,0:T(8,128)(2,1)S(1)} async-done(((bf16[16,128,128]{2,1,0:T(8,128)(2,1)}), bf16[16,128,128]{2,1,0:T(8,128)(2,1)S(1)}, u32[]{:S(2)}, u32[]{:S(2)}) %all-to-all-start.1) | async-done | bytes 524320 | tf_op jit(solution)/shard_map/all_to_all | solution.py:51
  84.9 16.2 %all-to-all-start = ((bf16[2,1,32,2,64,128]{5,3,4,0,1,2:T(2,128)(2,1)}), bf16[2,1,32,2,64,128]{5,3,4,0,1,2:T(2,128)(2,1)S(1)}, u32[]{:S(2)}, u32[]{:S(2)}) async-start(bf16[2,1,32,2,64,128]{5,3,4,0,1,2:T(2,128)(2,1)} %copy.117), calls=%async_computation | async-start | bytes 4194304 | tf_op jit(solution)/shard_map/all_to_all | solution.py:103
  101.2 0.8 fusion.56
  102.0 0.9 fusion.30
  103.5 2.3 collective-permute-start.1
  105.8 9.5 %collective-permute-start = (bf16[2,64,128]{2,1,0:T(8,128)(2,1)S(1)}, bf16[2,64,128]{2,1,0:T(8,128)(2,1)S(1)}, u32[]{:S(2)}, u32[]{:S(2)}) collective-permute-start(bf16[2,64,128]{2,1,0:T(8,128)(2,1)S(1)} %get-tuple-element.39), channel_id=1, source_target_pairs={{0,16},{16,32},{32,48},{48,64},{64,80},{80,96},{96,112},{112,128},... | collective-permute-start | bytes 98312 | tf_op jit(solution)/shard_map/ppermute | solution.py:17
  115.7 28.9 %collective-permute-done.1 = bf16[2,64,128]{2,1,0:T(8,128)(2,1)S(1)} collective-permute-done((bf16[2,64,128]{2,1,0:T(8,128)(2,1)S(1)}, bf16[2,64,128]{2,1,0:T(8,128)(2,1)S(1)}, u32[]{:S(2)}, u32[]{:S(2)}) %collective-permute-start.1) | collective-permute-done | bytes 32800 | tf_op jit(solution)/shard_map/ppermute | solution.py:19
  144.6 62.7 %collective-permute-done = bf16[2,64,128]{2,1,0:T(8,128)(2,1)S(1)} collective-permute-done((bf16[2,64,128]{2,1,0:T(8,128)(2,1)S(1)}, bf16[2,64,128]{2,1,0:T(8,128)(2,1)S(1)}, u32[]{:S(2)}, u32[]{:S(2)}) %collective-permute-start) | collective-permute-done | bytes 32800 | tf_op jit(solution)/shard_map/ppermute | solution.py:17
  207.4 0.8 fusion.36
  208.1 0.8 fusion.35
  208.9 0.8 fusion.34
  209.7 270.5 %all-reduce.6.cloned.1.call-done = bf16[2,2,64,128]{3,1,2,0:T(2,128)(2,1)} async-done(((bf16[2,2,64,128]{3,1,2,0:T(2,128)(2,1)}), bf16[2,2,64,128]{3,1,2,0:T(2,128)(2,1)}) %all-reduce.6.cloned.1.call-update) | async-done | bytes 65552 | tf_op jit(solution)/shard_map/psum | solution.py:96
  480.2 0.8 copy.110
  481.0 0.9 broadcast_dynamic-update-slice_fusion
  482.3 2.3 convolution_convert_fusion
  484.6 1.3 fusion.16
  486.1 1.1 constant_dynamic-update-slice_fusion
  487.2 2.8 fusion.65
  490.4 1.5 fusion.67
  491.9 1.0 fusion.63
  492.9 2.9 multiply_reduce_fusion
  495.8 1.8 fusion.15
  499.5 2.0 convert_bitcast_fusion
  501.4 3.6 copy.132
  505.1 12.3 %all-to-all-start.2 = ((bf16[2,1,32,2,64,128]{5,3,4,0,1,2:T(2,128)(2,1)}), bf16[2,1,32,2,64,128]{5,3,4,0,1,2:T(2,128)(2,1)S(1)}, u32[]{:S(2)}, u32[]{:S(2)}) async-start(bf16[2,1,32,2,64,128]{5,3,4,0,1,2:T(2,128)(2,1)} %copy.132), calls=%async_computation.2 | async-start | bytes 4194304 | tf_op jit(solution)/shard_map/all_to_all | solution.py:208
  517.7 1.4 convolution_multiply_fusion
  519.5 0.7 copy_dynamic-update-slice_fusion.1
  520.3 0.8 copy_dynamic-update-slice_fusion
  521.0 1.5 copy-done.1
  522.8 0.7 copy.169
  524.1 1.5 slice_bitcast_fusion.2
  525.7 2.4 collective-permute-start.3
  528.1 9.3 %collective-permute-start.2 = (bf16[2,1,1,64,128]{4,2,3,0,1:T(2,128)(2,1)S(1)}, bf16[2,1,1,64,128]{4,2,3,0,1:T(2,128)(2,1)S(1)}, u32[]{:S(2)}, u32[]{:S(2)}) collective-permute-start(bf16[2,1,1,64,128]{4,2,3,0,1:T(2,128)(2,1)S(1)} %get-tuple-element.35), channel_id=1, source_target_pairs={{0,16},{16,32},{32,48},{48,64},{64,80},{80,96},{96,112},{112,128},... | collective-permute-start | bytes 98312 | tf_op jit(solution)/shard_map/ppermute | solution.py:17
  537.6 1.0 fusion.29
  538.8 29.3 %collective-permute-done.3 = bf16[2,1,1,64,128]{4,2,3,0,1:T(2,128)(2,1)S(1)} collective-permute-done((bf16[2,1,1,64,128]{4,2,3,0,1:T(2,128)(2,1)S(1)}, bf16[2,1,1,64,128]{4,2,3,0,1:T(2,128)(2,1)S(1)}, u32[]{:S(2)}, u32[]{:S(2)}) %collective-permute-start.3) | collective-permute-done | bytes 32800 | tf_op jit(solution)/shard_map/ppermute | solution.py:19
  568.1 38.3 %collective-permute-done.2 = bf16[2,1,1,64,128]{4,2,3,0,1:T(2,128)(2,1)S(1)} collective-permute-done((bf16[2,1,1,64,128]{4,2,3,0,1:T(2,128)(2,1)S(1)}, bf16[2,1,1,64,128]{4,2,3,0,1:T(2,128)(2,1)S(1)}, u32[]{:S(2)}, u32[]{:S(2)}) %collective-permute-start.2) | collective-permute-done | bytes 32800 | tf_op jit(solution)/shard_map/ppermute | solution.py:17
  606.7 1.3 scatter-add.6
  608.3 1.3 scatter-add.9
  609.6 292.4 %all-reduce.8.cloned.1.call-done = bf16[2,2,64,128]{3,1,2,0:T(2,128)(2,1)} async-done(((bf16[2,2,64,128]{3,1,2,0:T(2,128)(2,1)}), bf16[2,2,64,128]{3,1,2,0:T(2,128)(2,1)}) %all-reduce.8.cloned.1.call-update) | async-done | bytes 65552 | tf_op jit(solution)/shard_map/psum | solution.py:185
  902.0 1.2 fusion.25
  903.2 3.0 convolution_convert_fusion.1
  906.2 1.9 fusion.26
  908.1 0.7 copy.134
  (65 shorter events, 8.0 us)
Async XLA Ops:
  8.0 481.9 %copy-start = (bf16[512,128]{1,0:T(8,128)(2,1)S(1)}, bf16[512,128]{1,0:T(8,128)(2,1)}, u32[]{:S(2)}) copy-start(bf16[512,128]{1,0:T(8,128)(2,1)} %param.10) | copy-start | bytes 393220
  8.0 62.5 %copy-start.7 = (bf16[512,128]{1,0:T(8,128)(2,1)S(1)}, bf16[512,128]{1,0:T(8,128)(2,1)}, u32[]{:S(2)}) copy-start(bf16[512,128]{1,0:T(8,128)(2,1)} %param.11) | copy-start | bytes 393220
  8.0 62.6 %copy-start.6 = (bf16[512,128]{1,0:T(8,128)(2,1)S(1)}, bf16[512,128]{1,0:T(8,128)(2,1)}, u32[]{:S(2)}) copy-start(bf16[512,128]{1,0:T(8,128)(2,1)} %param.12) | copy-start | bytes 393220
  60.4 24.5 %all-to-all-start.1 = ((bf16[16,128,128]{2,1,0:T(8,128)(2,1)}), bf16[16,128,128]{2,1,0:T(8,128)(2,1)S(1)}, u32[]{:S(2)}, u32[]{:S(2)}) async-start(bf16[16,128,128]{2,1,0:T(8,128)(2,1)} %bitcast.39), calls=%async_computation.1 | async-start | bytes 1048576 | tf_op jit(solution)/shard_map/all_to_all | solution.py:51
  84.9 399.7 %all-to-all-start = ((bf16[2,1,32,2,64,128]{5,3,4,0,1,2:T(2,128)(2,1)}), bf16[2,1,32,2,64,128]{5,3,4,0,1,2:T(2,128)(2,1)S(1)}, u32[]{:S(2)}, u32[]{:S(2)}) async-start(bf16[2,1,32,2,64,128]{5,3,4,0,1,2:T(2,128)(2,1)} %copy.117), calls=%async_computation | async-start | bytes 4194304 | tf_op jit(solution)/shard_map/all_to_all | solution.py:103
  101.1 379.0 %all-reduce.6.cloned.1.call-start = ((), (), s32[]{:S(2)}) async-start(), calls=%async_computation.3 | async-start | bytes 131072 | tf_op jit(solution)/shard_map/psum | solution.py:96
  103.0 379.3 %all-gather.5.cloned.1.call-start = ((), (), s32[]{:S(2)}) async-start(), calls=%async_computation.5 | async-start | bytes 2228224 | tf_op jit(solution)/shard_map/all_gather | solution.py:133
  103.5 41.1 %collective-permute-start.1 = (bf16[2,64,128]{2,1,0:T(8,128)(2,1)S(1)}, bf16[2,64,128]{2,1,0:T(8,128)(2,1)S(1)}, u32[]{:S(2)}, u32[]{:S(2)}) collective-permute-start(bf16[2,64,128]{2,1,0:T(8,128)(2,1)S(1)} %get-tuple-element.40), channel_id=1, source_target_pairs={{16,0},{32,16},{48,32},{64,48},{80,64},{96,80},{112,96},{128,112},... | collective-permute-start | bytes 98312 | tf_op jit(solution)/shard_map/ppermute | solution.py:19
  105.8 101.5 %collective-permute-start = (bf16[2,64,128]{2,1,0:T(8,128)(2,1)S(1)}, bf16[2,64,128]{2,1,0:T(8,128)(2,1)S(1)}, u32[]{:S(2)}, u32[]{:S(2)}) collective-permute-start(bf16[2,64,128]{2,1,0:T(8,128)(2,1)S(1)} %get-tuple-element.39), channel_id=1, source_target_pairs={{0,16},{16,32},{32,48},{48,64},{64,80},{80,96},{96,112},{112,128},... | collective-permute-start | bytes 98312 | tf_op jit(solution)/shard_map/ppermute | solution.py:17
  495.8 1.8 copy-start.2
  497.6 1.4 copy-start.4
  505.1 401.2 %all-to-all-start.2 = ((bf16[2,1,32,2,64,128]{5,3,4,0,1,2:T(2,128)(2,1)}), bf16[2,1,32,2,64,128]{5,3,4,0,1,2:T(2,128)(2,1)S(1)}, u32[]{:S(2)}, u32[]{:S(2)}) async-start(bf16[2,1,32,2,64,128]{5,3,4,0,1,2:T(2,128)(2,1)} %copy.132), calls=%async_computation.2 | async-start | bytes 4194304 | tf_op jit(solution)/shard_map/all_to_all | solution.py:208
  517.4 384.5 %all-reduce.8.cloned.1.call-start = ((), (), s32[]{:S(2)}) async-start(), calls=%async_computation.6 | async-start | bytes 131072 | tf_op jit(solution)/shard_map/psum | solution.py:185
  517.7 1.5 copy-start.3
  521.0 1.5 copy-start.1
  523.5 379.6 %all-gather.3.cloned.1.call-start = ((), (), s32[]{:S(2)}) async-start(), calls=%async_computation.4 | async-start | bytes 2228224 | tf_op jit(solution)/shard_map/all_gather | solution.py:127
  525.6 12.0 %copy-start.5 = (bf16[8,64,512]{2,1,0:T(8,128)(2,1)S(1)}, bf16[8,64,512]{2,1,0:T(8,128)(2,1)}, u32[]{:S(2)}) copy-start(bf16[8,64,512]{2,1,0:T(8,128)(2,1)} %copy-done.4) | copy-start | bytes 1572868
  525.7 42.4 %collective-permute-start.3 = (bf16[2,1,1,64,128]{4,2,3,0,1:T(2,128)(2,1)S(1)}, bf16[2,1,1,64,128]{4,2,3,0,1:T(2,128)(2,1)S(1)}, u32[]{:S(2)}, u32[]{:S(2)}) collective-permute-start(bf16[2,1,1,64,128]{4,2,3,0,1:T(2,128)(2,1)S(1)} %get-tuple-element.36), channel_id=1, source_target_pairs={{16,0},{32,16},{48,32},{64,48},{80,64},{96,80},{112,96},{128,112},... | collective-permute-start | bytes 98312 | tf_op jit(solution)/shard_map/ppermute | solution.py:19
  528.1 78.3 %collective-permute-start.2 = (bf16[2,1,1,64,128]{4,2,3,0,1:T(2,128)(2,1)S(1)}, bf16[2,1,1,64,128]{4,2,3,0,1:T(2,128)(2,1)S(1)}, u32[]{:S(2)}, u32[]{:S(2)}) collective-permute-start(bf16[2,1,1,64,128]{4,2,3,0,1:T(2,128)(2,1)S(1)} %get-tuple-element.35), channel_id=1, source_target_pairs={{0,16},{16,32},{32,48},{48,64},{64,80},{80,96},{96,112},{112,128},... | collective-permute-start | bytes 98312 | tf_op jit(solution)/shard_map/ppermute | solution.py:17
Sparse Core Ops, SparseCore 0:
  105.5 374.6 all-reduce.5
  523.6 378.2 all-reduce.7
Sparse Core Ops, SparseCore 1:
  105.4 144.2 all-gather.4
  526.8 144.5 all-gather.2
where the time goes:
time: 918 us; the launch traced here: 917 us
  waiting for transfers between devices  733 us (80%)
  starting transfers between devices  61 us (7%)
  blocking collectives  52.4 us (6%)
  local copies, waits for them, and re-layouts  27.2 us (3%)
  matrix products  22.2 us (2%)
  between operations  16 us (2%)
    psum x1, waiting for transfers between devices, per_device(): lax.psum(jnp.sum(near_terms[:, :, :, 3:5], axis=2).astype(jnp.bfloat16),...  292 us
    psum x1, waiting for transfers between devices, per_device(): lax.psum(global_part.astype(jnp.bfloat16), 'seq').astype(jnp.float32)  270 us
    ppermute x2, waiting for transfers between devices, with_halo(): lax.ppermute(tail, axis, [(i, (i + 1) % count) for i in range(count)])  101 us
    ppermute x2, waiting for transfers between devices, with_halo(): lax.ppermute(head, axis, [((i + 1) % count, i) for i in range(count)])  58.2 us
    all_gather x1, blocking collectives, per_device(): weight_cols = lax.all_gather(out_weight, 'seq', axis=0, tiled=True)  52.4 us
    ppermute x2, starting transfers between devices, with_halo(): lax.ppermute(tail, axis, [(i, (i + 1) % count) for i in range(count)])  18.8 us
  transfers between devices with their start and end apart: 11, of which 7 were waited for; matrix products, arithmetic and copies ran while one was open for 3% of the time, Pallas kernels for 0%

commit v1 on v0

v1 whole, which is shorter than its diff:
```python
import functools

import jax
import jax.numpy as jnp
from jax import lax
from jax.experimental import pallas as pl
from jax.experimental.pallas import tpu as pltpu
from jax.sharding import PartitionSpec as P

HEAD_DIM = 128
BLOCK = 64
SCALE = HEAD_DIM**-0.5
CAP = 2
VMEM_LIMIT = 48 * 1024 * 1024
MESH = pl.DeviceIdType.MESH
f32 = jnp.float32
bf16 = jnp.bfloat16


class Place:
    def __init__(self, dims):
        self.Z, self.P, self.Y, self.L = dims
        seq, dp = lax.axis_index("seq"), lax.axis_index("dp")
        self.seq, self.dp = seq, dp
        self.z, self.p = seq // self.P, seq % self.P
        self.y, self.l = dp // self.L, dp % self.L

    def at_z(self, j):
        return {"seq": (self.z + j) % self.Z * self.P + self.p, "dp": self.dp}

    def at_p(self, j):
        return {"seq": self.z * self.P + (self.p + j) % self.P, "dp": self.dp}

    def at_y(self, j):
        return {"seq": self.seq, "dp": (self.y + j) % self.Y * self.L + self.l}

    def at_l(self, j):
        return {"seq": self.seq, "dp": self.y * self.L + (self.l + j) % self.L}

    def at_s(self, j):
        return {"seq": (self.seq + j) % (self.Z * self.P), "dp": self.dp}

    def enter(self):
        partners = (
            [self.at_p(j) for j in range(1, self.P)]
            + [self.at_z(j) for j in range(1, self.Z)]
            + [self.at_y(j) for j in range(1, self.Y)]
            + [self.at_l(j) for j in range(1, self.L)]
            + [self.at_s(1), self.at_s(-1)]
        )
        barrier = pltpu.get_barrier_semaphore()
        for partner in partners:
            pl.semaphore_signal(barrier, inc=1, device_id=partner, device_id_type=MESH)
        pl.semaphore_wait(barrier, len(partners))


class Wire:
    def __init__(self, send_sems, recv_sems):
        self.send_sems, self.recv_sems = send_sems, recv_sems
        self.used = 0
        self.sent = []

    def send(self, src, dst, target):
        copy = pltpu.make_async_remote_copy(
            src_ref=src,
            dst_ref=dst,
            send_sem=self.send_sems.at[self.used],
            recv_sem=self.recv_sems.at[self.used],
            device_id=target,
            device_id_type=MESH,
        )
        self.used += 1
        copy.start()
        self.sent.append(copy)
        return copy

    def finish(self):
        for copy in self.sent:
            copy.wait_send()


def gather_kernel(
    dims, k, v, w, go, pick, gpick, gowner,
    halo, glob, rnd, wall, gctx,
    kvm, kvp, kv2, kblk, vblk, sb0, sb1, sb2, sb3, edge,
    gcand, ga, gmine, gb, gpiece, wcol, ps, pr, ysum, lr, send_sems, recv_sems,
):
    me = Place(dims)
    Z, PN, Y, L = dims
    wire = Wire(send_sems, recv_sems)
    blocks = k.shape[0] // BLOCK
    half = go.shape[0] // 2
    piece = glob.shape[1]

    kblk[...] = k[...].reshape(blocks, BLOCK, HEAD_DIM)
    vblk[...] = v[...].reshape(blocks, BLOCK, HEAD_DIM)
    edge[0, 0] = kblk[blocks - 1]
    edge[0, 1] = vblk[blocks - 1]
    edge[1, 0] = kblk[0]
    edge[1, 1] = vblk[0]
    for j in range(2):
        at = gpick[j]
        for part, source in ((0, kblk), (1, vblk)):
            rows = source[at].reshape(BLOCK // piece, piece, HEAD_DIM)
            first = (j * 2 + part) * (BLOCK // piece)
            gcand[first : first + BLOCK // piece] = rows
    me.enter()

    w_z = [wire.send(w, wcol.at[me.z], me.at_z(j)) for j in range(1, Z)]
    edges = [
        wire.send(edge.at[0], halo.at[0], me.at_s(1)),
        wire.send(edge.at[1], halo.at[1], me.at_s(-1)),
    ]
    g_a = [
        wire.send(gcand.at[(me.p + j) % PN], ga.at[me.p], me.at_p(j)) for j in range(1, PN)
    ]
    k_up = wire.send(kblk, kvm.at[0], me.at_z(1))
    v_down = wire.send(vblk, kvp.at[1], me.at_z(-1))
    v_up = wire.send(vblk, kvm.at[1], me.at_z(1))
    k_down = wire.send(kblk, kvp.at[0], me.at_z(-1))

    arrivals = []

    def pack(at, keys, values, buffer):
        for requester in range(PN):
            for c in range(CAP):
                block = pick[(at * PN + requester) * CAP + c]
                buffer[requester, c, 0] = keys(block)
                buffer[requester, c, 1] = values(block)
        rnd[at, pl.ds(me.p, 1)] = buffer[pl.ds(me.p, 1)]
        for j in range(1, PN):
            arrivals.append(
                wire.send(buffer.at[(me.p + j) % PN], rnd.at[at, me.p], me.at_p(j))
            )

    wcol[pl.ds(me.z, 1)] = w[...][None]
    ga[pl.ds(me.p, 1)] = gcand[pl.ds(me.p, 1)]
    for copy in w_z:
        copy.wait_recv()
    wall[:, pl.ds(me.p, 1)] = wcol[...][:, None]
    w_p = [wire.send(wcol, wall.at[:, me.p], me.at_p(j)) for j in range(1, PN)]

    for copy in g_a:
        copy.wait_recv()
    half_pieces = PN // 2
    own_half = (me.p // half_pieces) % 2
    owner_p = jnp.where(own_half == 0, gowner[0], gowner[1])
    gmine[...] = ga[owner_p]
    g_b = [wire.send(gmine, gb.at[j], me.at_z(j)) for j in range(1, Z)]

    pack(0, lambda b: kblk[b], lambda b: vblk[b], sb0)

    for copy in w_p:
        copy.wait_recv()
    chunk_z = Z // Y
    width = L * HEAD_DIM
    y_sends = []
    for part in range(2):
        rows = go[part * half : (part + 1) * half]
        for j in list(range(1, Y)) + [0]:
            to = (me.y + j) % Y
            weight = wall[pl.ds(to * chunk_z, chunk_z)].reshape(width, HEAD_DIM)
            terms = lax.dot_general(
                rows, weight, (((1,), (1,)), ((), ())), preferred_element_type=f32
            ).astype(bf16)
            for head in range(L):
                ps[part, j, head] = terms[:, head * HEAD_DIM : (head + 1) * HEAD_DIM]
            if j:
                y_sends.append(wire.send(ps.at[part, j], pr.at[part, j - 1], me.at_y(j)))

    for copy in g_b:
        copy.wait_recv()
    owner_z = jnp.where(own_half == 0, gowner[2], gowner[3])
    gb[0] = gmine[...]
    gpiece[...] = gb[owner_z]
    glob[pl.ds(me.p, 1)] = gpiece[...][None]
    g_c = [wire.send(gpiece, glob.at[me.p], me.at_p(j)) for j in range(1, PN)]

    k_up.wait_recv()
    k_far = wire.send(kvm.at[0], kv2.at[0], me.at_z(1))
    v_down.wait_recv()
    v_far = wire.send(kvp.at[1], kv2.at[1], me.at_z(-1))

    def y_stage(part):
        for copy in y_sends[part * (Y - 1) : (part + 1) * (Y - 1)]:
            copy.wait_recv()
        for head in range(L):
            total = ps[part, 0, head].astype(f32)
            for j in range(1, Y):
                total = total + pr[part, j - 1, head].astype(f32)
            ysum[part, head] = total.astype(bf16)
        return [
            wire.send(ysum.at[part, (me.l + j) % L], lr.at[part, j - 1], me.at_l(j))
            for j in range(1, L)
        ]

    v_up.wait_recv()
    pack(1, lambda b: kvm[0, b], lambda b: kvm[1, b], sb1)
    k_down.wait_recv()
    pack(2, lambda b: kvp[0, b], lambda b: kvp[1, b], sb2)
    l_sends = [y_stage(0), y_stage(1)]
    k_far.wait_recv()
    v_far.wait_recv()
    pack(3, lambda b: kv2[0, b], lambda b: kv2[1, b], sb3)
    for part in range(2):
        for copy in l_sends[part]:
            copy.wait_recv()
        total = ysum[part, pl.ds(me.l, 1)][0].astype(f32)
        for j in range(1, L):
            total = total + lr[part, j - 1].astype(f32)
        gctx[part * half : (part + 1) * half] = total.astype(bf16)
    for copy in edges + g_c + arrivals:
        copy.wait_recv()
    wire.finish()


def attend_kernel(
    q, k, v, halo, glob, rnd, gctx, slot_of, entry_of,
    ctx, dq, sb, own, edge, gsum,
    fr,
):
    blocks = q.shape[0] // BLOCK
    entries = 3 * blocks

    def window(b, part, source):
        before = halo[0, part] if b == 0 else source[(b - 1) * BLOCK : b * BLOCK]
        after = halo[1, part] if b == blocks - 1 else source[(b + 1) * BLOCK : (b + 2) * BLOCK]
        return [before, source[b * BLOCK : (b + 1) * BLOCK], after]

    def dot(a, b, dims):
        return lax.dot_general(a, b, (dims, ((), ())), preferred_element_type=f32)

    nt, nn, tn = ((1,), (1,)), ((1,), (0,)), ((0,), (0,))
    gk = [glob[0], glob[2]]
    gv = [glob[1], glob[3]]
    acc = {}
    total = [jnp.zeros((2 * BLOCK, HEAD_DIM), f32) for _ in range(2)]

    def settle(at):
        for part in range(2):
            term = acc.pop((at, part))
            if at < 0:
                edge[0, part] = term.astype(bf16)
            elif at >= blocks:
                edge[1, part] = term.astype(bf16)
            else:
                own[part, at] = term

    fr[entries] = jnp.zeros(fr.shape[1:], bf16)
    for b in range(blocks):
        rows = slice(b * BLOCK, (b + 1) * BLOCK)
        slots = [slot_of[b * 3 + i] for i in range(3)]
        keys = jnp.concatenate(window(b, 0, k) + gk + [rnd[s, 0] for s in slots], axis=0)
        values = jnp.concatenate(window(b, 1, v) + gv + [rnd[s, 1] for s in slots], axis=0)
        qb, gb = q[rows], gctx[rows]
        scores = dot(qb, keys, nt) * SCALE
        top = jnp.max(scores, axis=-1, keepdims=True)
        raised = jnp.exp(scores - top)
        probs32 = raised / jnp.sum(raised, axis=-1, keepdims=True)
        probs = probs32.astype(bf16)
        context = dot(probs, values, nn).astype(bf16)
        ctx[rows] = context
        delta = jnp.sum(gb.astype(f32) * context.astype(f32), axis=-1, keepdims=True)
        gprobs = dot(gb, values, nt)
        gscores = (probs32 * (gprobs - delta)).astype(bf16)
        dq[rows] = (dot(gscores, keys, nn) * SCALE).astype(bf16)
        for part, term in (
            (0, dot(gscores, qb, tn) * SCALE),
            (1, dot(probs, gb, tn)),
        ):
            for i in range(3):
                at = (b - 1 + i, part)
                piece = term[i * BLOCK : (i + 1) * BLOCK]
                acc[at] = acc[at] + piece if at in acc else piece
            total[part] = total[part] + term[3 * BLOCK : 5 * BLOCK]
            for i in range(3):
                fr[b * 3 + i, part] = term[(5 + i) * BLOCK : (6 + i) * BLOCK].astype(bf16)
        settle(b - 1)
    settle(blocks - 1)
    settle(blocks)
    for j in range(2):
        for part in range(2):
            gsum[j * 2 + part] = total[part][j * BLOCK : (j + 1) * BLOCK].astype(bf16)
    for slot in range(sb.shape[0]):
        sb[slot] = fr[entry_of[slot]]


def scatter_kernel(
    dims, ctx, wall, sb, own, edge, gsum, pickx, ghit,
    out, dk, dv,
    halo, ar0, ar1, ar2, ar3, p1, p2, p3, fm, fp, rm, rp,
    ga, gmine, gb, gpiece, gall, cr, send_sems, recv_sems,
):
    me = Place(dims)
    Z, PN, Y, L = dims
    wire = Wire(send_sems, recv_sems)
    blocks = own.shape[1]
    me.enter()

    order = (3, 1, 2, 0)
    landing = {0: ar0, 1: ar1, 2: ar2, 3: ar3}
    arrivals = {}

    def spread(at):
        arrivals[at] = [
            wire.send(sb.at[at, (me.p + j) % PN], landing[at].at[me.p], me.at_p(j))
            for j in range(1, PN)
        ]

    spread(3)
    g_a = [
        wire.send(gsum.at[(me.p + j) % PN], ga.at[me.p], me.at_p(j)) for j in range(1, PN)
    ]
    cr[pl.ds(me.y, 1), pl.ds(me.l, 1)] = ctx[...][None, None]
    l_in = [
        wire.send(ctx, cr.at[me.y, me.l], me.at_l(j)) for j in range(1, L)
    ]
    y_in = [wire.send(ctx, cr.at[me.y, me.l], me.at_y(j)) for j in range(1, Y)]
    edges = [
        wire.send(edge.at[0], halo.at[1], me.at_s(-1)),
        wire.send(edge.at[1], halo.at[0], me.at_s(1)),
    ]
    for at in order[1:]:
        spread(at)

    def gather_sum(at):
        landed = landing[at]
        landed[pl.ds(me.p, 1)] = sb[at, pl.ds(me.p, 1)]
        for copy in arrivals[at]:
            copy.wait_recv()
        rows, cols = blocks * 16, PN * CAP * 16
        row = lax.broadcasted_iota(jnp.int32, (rows, cols), 0)
        col = lax.broadcasted_iota(jnp.int32, (rows, cols), 1)
        wanted = jnp.broadcast_to(pickx[at : at + 1], (rows, cols))
        here = (wanted == row // 16) & (row % 16 == col % 16)
        select = jnp.where(here, 1.0, 0.0).astype(bf16)
        sums = []
        for part in range(2):
            pieces = []
            for r in range(BLOCK // 16):
                data = landed[:, :, part, r * 16 : (r + 1) * 16].reshape(cols, HEAD_DIM)
                pieces.append(
                    jnp.dot(select, data, preferred_element_type=f32).reshape(
                        blocks, 16, HEAD_DIM
                    )
                )
            sums.append(jnp.concatenate(pieces, axis=1))
        return sums

    far = gather_sum(3)
    p2[0] = far[0].astype(bf16)
    p2[1] = far[1].astype(bf16)
    far_up = wire.send(p2.at[0], fm, me.at_z(1))
    far_down = wire.send(p2.at[1], fp, me.at_z(-1))

    for copy in g_a:
        copy.wait_recv()
    ga[pl.ds(me.p, 1)] = gsum[pl.ds(me.p, 1)]
    gmine[...] = jnp.sum(ga[...].astype(f32), axis=0).astype(bf16)
    g_b = [wire.send(gmine, gb.at[j - 1], me.at_z(j)) for j in range(1, Z)]

    down = gather_sum(1)
    p3[0] = down[0].astype(bf16)
    k_down = wire.send(p3.at[0], rp.at[0], me.at_z(-1))
    up = gather_sum(2)
    p1[1] = up[1].astype(bf16)
    v_up = wire.send(p1.at[1], rm.at[1], me.at_z(1))
    for j in range(1, L):
        l_in[j - 1].wait_recv()
        source = (me.l + L - j) % L
        for i in range(1, Y):
            y_in.append(wire.send(cr.at[me.y, source], cr.at[me.y, source], me.at_y(i)))
    far_up.wait_recv()
    p1[0] = (up[0] + fm[...].astype(f32)).astype(bf16)
    k_up = wire.send(p1.at[0], rm.at[0], me.at_z(1))
    far_down.wait_recv()
    p3[1] = (down[1] + fp[...].astype(f32)).astype(bf16)
    v_down = wire.send(p3.at[1], rp.at[1], me.at_z(-1))

    for copy in g_b:
        copy.wait_recv()
    gpiece[...] = (
        gmine[...].astype(f32) + jnp.sum(gb[...].astype(f32), axis=0)
    ).astype(bf16)
    gall[pl.ds(me.p, 1)] = gpiece[...][None]
    g_c = [wire.send(gpiece, gall.at[me.p], me.at_p(j)) for j in range(1, PN)]

    totals = gather_sum(0)
    for copy in y_in:
        copy.wait_recv()
    result = jnp.zeros(out.shape, f32)
    heads_z = Y * L // Z
    for y in range(Y):
        for l in range(L):
            head = y * L + l
            weight = wall[head * HEAD_DIM : (head + 1) * HEAD_DIM]
            result = result + jnp.dot(cr[y, l], weight, preferred_element_type=f32)
    out[...] = result.astype(bf16)

    for copy in edges + g_c:
        copy.wait_recv()
    k_down.wait_recv()
    v_up.wait_recv()
    k_up.wait_recv()
    v_down.wait_recv()
    everyone = gall[...].reshape(2, 2, BLOCK, HEAD_DIM).astype(f32)
    for part, target in ((0, dk), (1, dv)):
        total = totals[part] + own[part]
        total = total + (rm[part].astype(f32) + rp[part].astype(f32))
        for b in range(blocks):
            one = total[b]
            for j in range(2):
                hit = ghit[j] == b
                one = one + jnp.where(hit, everyone[j, part], 0.0)
            if b == 0:
                one = one + halo[0, part].astype(f32)
            if b == blocks - 1:
                one = one + halo[1, part].astype(f32)
            target[b * BLOCK : (b + 1) * BLOCK] = one.astype(bf16)
    wire.finish()


def plan(dims, pattern, blocks):
    me = Place(dims)
    Z, PN, Y, L = dims
    seqs = Z * PN
    head = lax.dynamic_slice_in_dim(pattern, me.dp, 1, 0)[0]
    shared = head[0, :2]
    entries = 3 * blocks
    mine = lax.dynamic_slice_in_dim(head, me.z * PN * blocks, PN * blocks, 0)
    wanted = mine[:, 2:].reshape(PN, entries)
    owner = wanted // blocks
    e = jnp.arange(entries, dtype=jnp.int32)
    same = owner[:, :, None] == owner[:, None, :]
    rank = jnp.sum((same & (e[None, :] < e[:, None])).astype(jnp.int32), axis=-1)
    rel = jnp.array([0, Z - 1, 1, 2], jnp.int32)
    places = (me.z + rel) % Z
    c = jnp.arange(CAP, dtype=jnp.int32)
    column = places * PN + me.p
    hit = (owner[None, :, None, :] == column[:, None, None, None]) & (
        rank[None, :, None, :] == c[None, None, :, None]
    )
    pick = jnp.sum(jnp.where(hit, wanted[None, :, None, :] % blocks + 1, 0), axis=-1) - 1
    my_owner = lax.dynamic_slice_in_dim(owner, me.p, 1, 0)[0]
    my_rank = lax.dynamic_slice_in_dim(rank, me.p, 1, 0)[0]
    back = (my_owner // PN - me.z) % Z
    order_of = jnp.where(back == 0, 0, jnp.where(back == 1, 2, jnp.where(back == 2, 3, 1)))
    slot_of = (order_of * PN + my_owner % PN) * CAP + my_rank
    slots = jnp.arange(4 * PN * CAP, dtype=jnp.int32)
    entry_of = entries - jnp.sum(
        jnp.where(slot_of[None, :] == slots[:, None], entries - e[None, :], 0), axis=-1
    )
    g_seq = shared // blocks
    g_owner = jnp.concatenate([g_seq % PN, (me.z - g_seq // PN) % Z])
    ghit = jnp.where(g_seq == me.seq, shared % blocks, -1)
    return pick, slot_of, entry_of, shared % blocks, g_owner, ghit


def vmem():
    return pl.BlockSpec(memory_space=pltpu.VMEM)


def smem():
    return pl.BlockSpec(memory_space=pltpu.SMEM)


def per_device(dims, queries, keys, values, out_weight, grad_out, pattern):
    Z, PN, Y, L = dims
    tokens = queries.shape[0]
    blocks = tokens // BLOCK
    rows = out_weight.shape[0]
    piece = 4 * BLOCK // PN
    block = (BLOCK, HEAD_DIM)
    pair = (2,) + block
    half = tokens // 2
    shape = jax.ShapeDtypeStruct
    pick, slot_of, entry_of, g_pick, g_owner, ghit = plan(dims, pattern, blocks)

    gather_sems = 3 + 2 + 7 + 4 + 7 * 4 + 7 + 3 + 6 + 7 + 2 + 6 + 8
    halo, glob, rnd, wall, gctx = pl.pallas_call(
        functools.partial(gather_kernel, dims),
        out_shape=(
            shape((2,) + pair, bf16),
            shape((PN, piece, HEAD_DIM), bf16),
            shape((4, PN, CAP) + pair, bf16),
            shape((Z, PN, rows, HEAD_DIM), bf16),
            shape((tokens, HEAD_DIM), bf16),
        ),
        in_specs=[vmem()] * 4 + [smem()] * 3,
        out_specs=(vmem(),) * 5,
        scratch_shapes=[
            pltpu.VMEM((2, blocks) + block, bf16),
            pltpu.VMEM((2, blocks) + block, bf16),
            pltpu.VMEM((2, blocks) + block, bf16),
            pltpu.VMEM((blocks,) + block, bf16),
            pltpu.VMEM((blocks,) + block, bf16),
            pltpu.VMEM((PN, CAP) + pair, bf16),
            pltpu.VMEM((PN, CAP) + pair, bf16),
            pltpu.VMEM((PN, CAP) + pair, bf16),
            pltpu.VMEM((PN, CAP) + pair, bf16),
            pltpu.VMEM((2,) + pair, bf16),
            pltpu.VMEM((PN, piece, HEAD_DIM), bf16),
            pltpu.VMEM((PN, piece, HEAD_DIM), bf16),
            pltpu.VMEM((piece, HEAD_DIM), bf16),
            pltpu.VMEM((Z, piece, HEAD_DIM), bf16),
            pltpu.VMEM((piece, HEAD_DIM), bf16),
            pltpu.VMEM((Z, rows, HEAD_DIM), bf16),
            pltpu.VMEM((2, Y, L, half, HEAD_DIM), bf16),
            pltpu.VMEM((2, Y - 1, L, half, HEAD_DIM), bf16),
            pltpu.VMEM((2, L, half, HEAD_DIM), bf16),
            pltpu.VMEM((2, L - 1, half, HEAD_DIM), bf16),
            pltpu.SemaphoreType.DMA((gather_sems,)),
            pltpu.SemaphoreType.DMA((gather_sems,)),
        ],
        compiler_params=pltpu.CompilerParams(
            collective_id=0, has_side_effects=True, vmem_limit_bytes=VMEM_LIMIT
        ),
    )(keys, values, out_weight, grad_out, jnp.maximum(pick, 0).reshape(-1), g_pick, g_owner)

    slots = 4 * PN * CAP
    ctx, dq, sb, own, edge, gsum = pl.pallas_call(
        attend_kernel,
        out_shape=(
            shape((tokens, HEAD_DIM), bf16),
            shape((tokens, HEAD_DIM), bf16),
            shape((slots,) + pair, bf16),
            shape((2, blocks) + block, f32),
            shape((2,) + pair, bf16),
            shape((4,) + block, bf16),
        ),
        in_specs=[vmem()] * 7 + [smem()] * 2,
        out_specs=(vmem(),) * 6,
        scratch_shapes=[pltpu.VMEM((3 * blocks + 1,) + pair, bf16)],
        compiler_params=pltpu.CompilerParams(vmem_limit_bytes=VMEM_LIMIT),
    )(
        queries, keys, values, halo, glob.reshape((4,) + block),
        rnd.reshape((slots,) + pair), gctx, slot_of, entry_of,
    )

    scatter_sems = 7 * 4 + 7 + 3 + 12 + 2 + 2 + 3 + 4 + 7 + 8
    landing = pltpu.VMEM((PN, CAP) + pair, bf16)
    half_sum = pltpu.VMEM((blocks,) + block, bf16)
    whole_sum = pltpu.VMEM((2, blocks) + block, bf16)
    out, dk, dv = pl.pallas_call(
        functools.partial(scatter_kernel, dims),
        out_shape=(shape((tokens, HEAD_DIM), bf16),) * 3,
        in_specs=[vmem()] * 7 + [smem()],
        out_specs=(vmem(),) * 3,
        scratch_shapes=[
            pltpu.VMEM((2,) + pair, bf16),
            landing, landing, landing, landing,
            whole_sum, whole_sum, whole_sum, half_sum, half_sum, whole_sum, whole_sum,
            pltpu.VMEM((PN, piece, HEAD_DIM), bf16),
            pltpu.VMEM((piece, HEAD_DIM), bf16),
            pltpu.VMEM((Z - 1, piece, HEAD_DIM), bf16),
            pltpu.VMEM((piece, HEAD_DIM), bf16),
            pltpu.VMEM((PN, piece, HEAD_DIM), bf16),
            pltpu.VMEM((Y, L, tokens, HEAD_DIM), bf16),
            pltpu.SemaphoreType.DMA((scatter_sems,)),
            pltpu.SemaphoreType.DMA((scatter_sems,)),
        ],
        compiler_params=pltpu.CompilerParams(
            collective_id=1, has_side_effects=True, vmem_limit_bytes=VMEM_LIMIT
        ),
    )(
        ctx, wall.reshape(-1, HEAD_DIM), sb.reshape((4, PN, CAP) + pair), own, edge,
        gsum.reshape(PN, piece, HEAD_DIM), jnp.repeat(pick.reshape(4, PN * CAP), 16, axis=1),
        ghit,
    )
    return out, dq, dk, dv


def solution(mesh, planes=8, lines=4):
    seq, dp = mesh.shape["seq"], mesh.shape["dp"]
    dims = (seq // planes, planes, dp // lines, lines)
    tile = P("seq", "dp")
    return jax.shard_map(
        functools.partial(per_device, dims),
        mesh=mesh,
        in_specs=(tile,) * 5 + (P(),),
        out_specs=(tile,) * 4,
        check_vma=False,
    )
```

time: 918 us -> 148 us (0.16)
  the two profiles are of different devices: /device:TPU:7 before, /device:TPU:33 now
where the time goes in v1:
time: 148 us
  Pallas kernels  138 us (93%)
  local copies, waits for them, and re-layouts  8.07 us (5%)
  other arithmetic  1.55 us (1%)
    pallas_call x1, Pallas kernels, per_device(): pl.pallas_call(functools.partial(gather_kernel, dims), out_shape=(shape((...  69.4 us
    pallas_call x1, Pallas kernels, per_device(): pl.pallas_call(functools.partial(scatter_kernel, dims), out_shape=(shape(...  61.6 us
    unnamed x17, local copies, waits for them, and re-layouts  7.14 us
    pallas_call x1, Pallas kernels, per_device(): pl.pallas_call(attend_kernel, out_shape=(shape((tokens, HEAD_DIM), bf16),...  6.72 us

profile of v1, /device:TPU:33, one launch (start us, length us, event | category | flops | bytes accessed | tf_op | source)
XLA Modules:
  0.0 148.1 jit_solution(16248932207557108436)
XLA Ops:
  0.6 0.0 copy-start
  0.7 0.8 copy-done
  1.5 0.1 constant_dynamic-slice_fusion.3
  1.7 0.1 slice_reduce_fusion
  1.8 0.7 fusion.7
  2.5 0.1 copy.30
  2.6 0.1 reshape.186
  2.7 0.3 convert_reduce_fusion
  3.1 0.1 broadcast_compare_fusion
  3.2 0.2 select_reduce_fusion
  3.4 0.1 select_reduce_fusion.1
  3.5 0.1 copy.34
  3.6 0.1 copy.35
  3.7 0.1 copy.32
  3.8 0.1 max.12.pick
  3.9 0.1 broadcast_in_dim.58
  4.0 0.1 reshape.192.pickx
  4.1 0.0 copy-start.1
  4.1 0.9 copy-done.1
  5.0 0.0 copy-start.2
  5.0 0.9 copy-done.2
  5.9 0.0 copy-start.4
  5.9 0.9 copy-done.4
  6.8 0.0 copy-start.5
  6.8 0.7 copy-done.5
  7.5 69.4 %shard_map.102 = (bf16[2,2,64,128]{3,2,1,0:T(8,128)(2,1)S(1)}, bf16[8,32,128]{2,1,0:T(8,128)(2,1)S(1)}, bf16[4,8,2,2,64,128]{5,4,3,2,1,0:T(8,128)(2,1)S(1)}, bf1...) custom-call(bf16[512,128]{1,0:T(8,128)(2,1)S(1)} %copy-done.1, bf16[512,128]{1,0:T(8,128)(2,1)S(1)} %copy-done.2, ...), custom_call_target="tpu_custom_call" | custom-call | tf_op jit(solution)/shard_map/pallas_call | solution.py:480
  76.9 0.0 copy-start.3
  76.9 0.9 copy-done.3
  77.8 6.7 %shard_map.103 = (bf16[512,128]{1,0:T(8,128)(2,1)S(1)}, bf16[512,128]{1,0:T(8,128)(2,1)}, bf16[64,2,64,128]{3,2,1,0:T(8,128)(2,1)S(1)}, f32[2,8,64,128]{3,2,1,0:...) custom-call(bf16[512,128]{1,0:T(8,128)(2,1)S(1)} %copy-done.3, ...), custom_call_target="tpu_custom_call" | custom-call | tf_op jit(solution)/shard_map/pallas_call | solution.py:521
  84.6 61.6 %shard_map.104 = (bf16[512,128]{1,0:T(8,128)(2,1)S(1)}, bf16[512,128]{1,0:T(8,128)(2,1)S(1)}, bf16[512,128]{1,0:T(8,128)(2,1)S(1)}) custom-call(bf16[512,128]{1,0:T(8,128)(2,1)S(1)} %get-tuple-element.22.ctx, bf16[2048,128]{1,0:T(8,128)(2,1)S(1)} %bitcast.31, bf16[4,8,2,2,64,128]{5,4,3,2,1,0:T(8,128)(2,1)S(1)} %bitcast.30, ...), custom_call_target="tpu_custom_call" | custom-call | tf_op jit(solution)/shard_map/pallas_call | solution.py:544
  146.1 0.7 copy.48
  146.8 0.7 copy.49
  147.4 0.7 copy.50
  (14 shorter events, 0.2 us)
Async XLA Ops:
  0.6 0.9 copy-start
  4.1 0.9 copy-start.1
  5.0 0.9 copy-start.2
  5.9 0.9 copy-start.4
  6.8 0.7 copy-start.5
  76.9 0.9 copy-start.3

commit v2 on v1

v2 whole, which is shorter than its diff:
```python
import functools

import jax
import jax.numpy as jnp
from jax import lax
from jax.experimental import pallas as pl
from jax.experimental.pallas import tpu as pltpu
from jax.sharding import PartitionSpec as P

HEAD_DIM = 128
BLOCK = 64
SCALE = HEAD_DIM**-0.5
CAP = 2
VMEM_LIMIT = 48 * 1024 * 1024
MESH = pl.DeviceIdType.MESH
f32 = jnp.float32
bf16 = jnp.bfloat16


class Place:
    def __init__(self, dims):
        self.Z, self.P, self.Y, self.L = dims
        seq, dp = lax.axis_index("seq"), lax.axis_index("dp")
        self.seq, self.dp = seq, dp
        self.z, self.p = seq // self.P, seq % self.P
        self.y, self.l = dp // self.L, dp % self.L

    def at_z(self, j):
        return {"seq": (self.z + j) % self.Z * self.P + self.p, "dp": self.dp}

    def at_p(self, j):
        return {"seq": self.z * self.P + (self.p + j) % self.P, "dp": self.dp}

    def at_y(self, j):
        return {"seq": self.seq, "dp": (self.y + j) % self.Y * self.L + self.l}

    def at_l(self, j):
        return {"seq": self.seq, "dp": self.y * self.L + (self.l + j) % self.L}

    def at_s(self, j):
        return {"seq": (self.seq + j) % (self.Z * self.P), "dp": self.dp}

    def enter(self, extra=()):
        partners = (
            [self.at_p(j) for j in range(1, self.P)]
            + [self.at_z(j) for j in range(1, self.Z)]
            + [self.at_y(j) for j in range(1, self.Y)]
            + [self.at_l(j) for j in range(1, self.L)]
            + [self.at_s(1), self.at_s(-1)]
        )
        partners += list(extra)
        barrier = pltpu.get_barrier_semaphore()
        for partner in partners:
            pl.semaphore_signal(barrier, inc=1, device_id=partner, device_id_type=MESH)
        pl.semaphore_wait(barrier, len(partners))


class Wire:
    def __init__(self, send_sems, recv_sems):
        self.send_sems, self.recv_sems = send_sems, recv_sems
        self.used = 0
        self.sent = []

    def send(self, src, dst, target):
        copy = pltpu.make_async_remote_copy(
            src_ref=src,
            dst_ref=dst,
            send_sem=self.send_sems.at[self.used],
            recv_sem=self.recv_sems.at[self.used],
            device_id=target,
            device_id_type=MESH,
        )
        self.used += 1
        copy.start()
        self.sent.append(copy)
        return copy

    def done(self, *copies):
        self.sent = [copy for copy in self.sent if not any(copy is c for c in copies)]

    def finish(self):
        for copy in self.sent:
            copy.wait_send()


def weight_route(me, dims, rows):
    seqs, heads = dims[0] * dims[1], dims[2] * dims[3]
    per_head = HEAD_DIM // rows
    shift = seqs // 2
    target = {
        "seq": (me.seq % per_head * heads + me.dp + shift) % seqs,
        "dp": me.seq // per_head,
    }
    tile = (me.seq + shift) % seqs
    source = {"seq": me.dp * per_head + tile // heads, "dp": tile % heads}
    return target, source


def gather_kernel(
    dims, k, v, w, go, pick, gpick, gowner,
    halo, glob, rnd, wh, gctx,
    km, vm, kp, vp, k2, v2, kblk, vblk, sb0, sb1, sb2, sb3, edge,
    gcand, ga, gmine, gb, gpiece, wmine, wcol, wall, gog, send_sems, recv_sems,
):
    me = Place(dims)
    Z, PN, Y, L = dims
    wire = Wire(send_sems, recv_sems)
    blocks = k.shape[0] // BLOCK
    piece = glob.shape[1]
    rows = w.shape[0]
    w_target, w_source = weight_route(me, dims, rows)

    kblk[...] = k[...].reshape(blocks, BLOCK, HEAD_DIM)
    vblk[...] = v[...].reshape(blocks, BLOCK, HEAD_DIM)
    edge[0, 0] = kblk[blocks - 1]
    edge[0, 1] = vblk[blocks - 1]
    edge[1, 0] = kblk[0]
    edge[1, 1] = vblk[0]
    for j in range(2):
        at = gpick[j]
        for part, source in ((0, kblk), (1, vblk)):
            first = (j * 2 + part) * (BLOCK // piece)
            gcand[first : first + BLOCK // piece] = source[at].reshape(
                BLOCK // piece, piece, HEAD_DIM
            )
    me.enter([w_source])

    w_in = wire.send(w, wmine, w_target)
    k_up = wire.send(kblk, km, me.at_z(1))
    k_down = wire.send(kblk, kp, me.at_z(-1))
    l_in = [wire.send(go, gog.at[me.y, me.l], me.at_l(j)) for j in range(1, L)]
    y_in = [wire.send(go, gog.at[me.y, me.l], me.at_y(j)) for j in range(1, Y)]
    g_a = [
        wire.send(gcand.at[(me.p + j) % PN], ga.at[me.p], me.at_p(j)) for j in range(1, PN)
    ]
    edges = [
        wire.send(edge.at[0], halo.at[0], me.at_s(1)),
        wire.send(edge.at[1], halo.at[1], me.at_s(-1)),
    ]
    gog[pl.ds(me.y, 1), pl.ds(me.l, 1)] = go[...][None, None]
    arrivals = []

    def pack(at, part, source, buffer):
        for requester in range(PN):
            for c in range(CAP):
                buffer[part, requester, c] = source(pick[(at * PN + requester) * CAP + c])
        rnd[at, part, pl.ds(me.p, 1)] = buffer[part, pl.ds(me.p, 1)]
        for j in range(1, PN):
            arrivals.append(
                wire.send(buffer.at[part, (me.p + j) % PN], rnd.at[at, part, me.p], me.at_p(j))
            )

    pack(0, 0, lambda b: kblk[b], sb0)
    pack(0, 1, lambda b: vblk[b], sb0)

    w_in.wait_recv()
    w_z = [wire.send(wmine, wcol.at[me.z], me.at_z(j)) for j in range(1, Z)]
    wcol[pl.ds(me.z, 1)] = wmine[...][None]

    ga[pl.ds(me.p, 1)] = gcand[pl.ds(me.p, 1)]
    for copy in g_a:
        copy.wait_recv()
    own_half = (me.p // (PN // 2)) % 2
    gmine[...] = ga[jnp.where(own_half == 0, gowner[0], gowner[1])]
    g_b = [wire.send(gmine, gb.at[j], me.at_z(j)) for j in range(1, Z)]

    for copy in w_z:
        copy.wait_recv()
    wall[pl.ds(me.p, 1)] = wcol[...][None]
    w_p = [wire.send(wcol, wall.at[me.p], me.at_p(j)) for j in range(1, PN)]

    gb[0] = gmine[...]
    for copy in g_b:
        copy.wait_recv()
    gpiece[...] = gb[jnp.where(own_half == 0, gowner[2], gowner[3])]
    glob[pl.ds(me.p, 1)] = gpiece[...][None]
    g_c = [wire.send(gpiece, glob.at[me.p], me.at_p(j)) for j in range(1, PN)]

    for j in range(1, L):
        l_in[j - 1].wait_recv()
        source = (me.l + L - j) % L
        for i in range(1, Y):
            y_in.append(wire.send(gog.at[me.y, source], gog.at[me.y, source], me.at_y(i)))

    k_up.wait_send()
    k_down.wait_send()
    wire.done(k_up, k_down)
    v_up = wire.send(vblk, vm, me.at_z(1))
    v_down = wire.send(vblk, vp, me.at_z(-1))

    low, high = pl.ds(0, blocks // 2), pl.ds(blocks // 2, blocks - blocks // 2)

    def forward(lower, upper, far):
        return [
            wire.send(lower.at[low], far.at[low], me.at_z(1)),
            wire.send(upper.at[high], far.at[high], me.at_z(-1)),
        ]

    k_up.wait_recv()
    k_down.wait_recv()
    k_far = forward(km, kp, k2)
    pack(1, 0, lambda b: km[b], sb1)
    pack(2, 0, lambda b: kp[b], sb2)
    v_up.wait_recv()
    v_down.wait_recv()
    v_far = forward(vm, vp, v2)
    for copy in k_far:
        copy.wait_recv()
    pack(1, 1, lambda b: vm[b], sb1)
    pack(2, 1, lambda b: vp[b], sb2)
    pack(3, 0, lambda b: k2[b], sb3)
    for copy in v_far:
        copy.wait_recv()
    pack(3, 1, lambda b: v2[b], sb3)

    for copy in w_p + y_in:
        copy.wait_recv()
    project(dims, rows, wall, gog, wh, gctx)
    for copy in edges + g_c + arrivals:
        copy.wait_recv()
    wire.finish()


def project(dims, rows, wall, gog, wh, gctx):
    Z, PN, Y, L = dims
    seqs, heads = Z * PN, Y * L
    total = jnp.zeros(gctx.shape, f32)
    for d in range(heads):
        tiles = []
        for i in range(HEAD_DIM // rows):
            slot = (i * heads + d + seqs // 2) % seqs
            tiles.append(wall[slot % PN, slot // PN])
        weight = jnp.concatenate(tiles, axis=0)
        wh[d] = weight
        total = total + lax.dot_general(
            gog[d // L, d % L], weight, (((1,), (1,)), ((), ())), preferred_element_type=f32
        )
    gctx[...] = total.astype(bf16)


def attend_kernel(
    q, k, v, halo, glob, rnd, gctx, slot_of, entry_of,
    ctx, dq, sb, own, edge, gsum,
    fr,
):
    blocks = q.shape[0] // BLOCK
    entries = 3 * blocks
    skip = rnd.shape[0] // 8

    def window(b, part, source):
        before = halo[0, part] if b == 0 else source[(b - 1) * BLOCK : b * BLOCK]
        after = halo[1, part] if b == blocks - 1 else source[(b + 1) * BLOCK : (b + 2) * BLOCK]
        return [before, source[b * BLOCK : (b + 1) * BLOCK], after]

    def dot(a, b, dims):
        return lax.dot_general(a, b, (dims, ((), ())), preferred_element_type=f32)

    nt, nn, tn = ((1,), (1,)), ((1,), (0,)), ((0,), (0,))
    gk = [glob[0], glob[2]]
    gv = [glob[1], glob[3]]
    acc = {}
    total = [jnp.zeros((2 * BLOCK, HEAD_DIM), f32) for _ in range(2)]

    def settle(at):
        for part in range(2):
            term = acc.pop((at, part))
            if at < 0:
                edge[0, part] = term.astype(bf16)
            elif at >= blocks:
                edge[1, part] = term.astype(bf16)
            else:
                own[part, at] = term

    fr[entries] = jnp.zeros(fr.shape[1:], bf16)
    for b in range(blocks):
        rows = slice(b * BLOCK, (b + 1) * BLOCK)
        slots = [slot_of[b * 3 + i] for i in range(3)]
        keys = jnp.concatenate(window(b, 0, k) + gk + [rnd[s] for s in slots], axis=0)
        values = jnp.concatenate(window(b, 1, v) + gv + [rnd[s + skip] for s in slots], axis=0)
        qb, gb = q[rows], gctx[rows]
        scores = dot(qb, keys, nt) * SCALE
        top = jnp.max(scores, axis=-1, keepdims=True)
        raised = jnp.exp(scores - top)
        probs32 = raised / jnp.sum(raised, axis=-1, keepdims=True)
        probs = probs32.astype(bf16)
        context = dot(probs, values, nn).astype(bf16)
        ctx[rows] = context
        delta = jnp.sum(gb.astype(f32) * context.astype(f32), axis=-1, keepdims=True)
        gprobs = dot(gb, values, nt)
        gscores = (probs32 * (gprobs - delta)).astype(bf16)
        dq[rows] = (dot(gscores, keys, nn) * SCALE).astype(bf16)
        for part, term in (
            (0, dot(gscores, qb, tn) * SCALE),
            (1, dot(probs, gb, tn)),
        ):
            for i in range(3):
                at = (b - 1 + i, part)
                piece = term[i * BLOCK : (i + 1) * BLOCK]
                acc[at] = acc[at] + piece if at in acc else piece
            total[part] = total[part] + term[3 * BLOCK : 5 * BLOCK]
            for i in range(3):
                fr[b * 3 + i, part] = term[(5 + i) * BLOCK : (6 + i) * BLOCK].astype(bf16)
        settle(b - 1)
    settle(blocks - 1)
    settle(blocks)
    for j in range(2):
        for part in range(2):
            gsum[j * 2 + part] = total[part][j * BLOCK : (j + 1) * BLOCK].astype(bf16)
    for at in range(4):
        for slot in range(skip):
            for part in range(2):
                sb[(at * 2 + part) * skip + slot] = fr[entry_of[at * skip + slot], part]


def scatter_kernel(
    dims, ctx, wh, sb, own, edge, gsum, pickx, ghit,
    out, dk, dv,
    halo, ar0, ar1, ar2, ar3, p1, p2, p3, fm, fp, rm, rp,
    ga, gmine, gb, gpiece, gall, ps, pr, ysum, lr, send_sems, recv_sems,
):
    me = Place(dims)
    Z, PN, Y, L = dims
    wire = Wire(send_sems, recv_sems)
    blocks = own.shape[1]
    half = ctx.shape[0] // 2
    me.enter()

    landing = {0: ar0, 1: ar1, 2: ar2, 3: ar3}
    arrivals = {}

    def spread(at, part):
        arrivals[at, part] = [
            wire.send(sb.at[at, part, (me.p + j) % PN], landing[at].at[part, me.p], me.at_p(j))
            for j in range(1, PN)
        ]

    def arrived(at, part):
        for copy in arrivals[at, part]:
            copy.wait_recv()

    def selection(at):
        rows, cols = blocks * 16, PN * CAP * 16
        row = lax.broadcasted_iota(jnp.int32, (rows, cols), 0)
        col = lax.broadcasted_iota(jnp.int32, (rows, cols), 1)
        wanted = jnp.broadcast_to(pickx[at : at + 1], (rows, cols))
        here = (wanted == row // 16) & (row % 16 == col % 16)
        return jnp.where(here, 1.0, 0.0).astype(bf16)

    def gather_sum(at, part, select):
        landed = landing[at]
        landed[part, pl.ds(me.p, 1)] = sb[at, part, pl.ds(me.p, 1)]
        pieces = []
        for r in range(BLOCK // 16):
            data = landed[part, :, :, r * 16 : (r + 1) * 16].reshape(-1, HEAD_DIM)
            terms = jnp.dot(select, data, preferred_element_type=f32)
            pieces.append(terms.reshape(blocks, 16, HEAD_DIM))
        return jnp.concatenate(pieces, axis=1)

    spread(3, 0)
    spread(3, 1)
    g_a = [
        wire.send(gsum.at[(me.p + j) % PN], ga.at[me.p], me.at_p(j)) for j in range(1, PN)
    ]
    edges = [
        wire.send(edge.at[0], halo.at[1], me.at_s(-1)),
        wire.send(edge.at[1], halo.at[0], me.at_s(1)),
    ]

    y_sends = []
    for part in range(2):
        rows = ctx[part * half : (part + 1) * half]
        for j in list(range(1, Y)) + [0]:
            to = (me.y + j) % Y
            for l in range(L):
                ps[part, j, l] = jnp.dot(
                    rows, wh[to * L + l], preferred_element_type=f32
                ).astype(bf16)
            if j:
                y_sends.append(wire.send(ps.at[part, j], pr.at[part, j - 1], me.at_y(j)))

    def y_stage(part):
        for copy in y_sends[part * (Y - 1) : (part + 1) * (Y - 1)]:
            copy.wait_recv()
        for l in range(L):
            total = ps[part, 0, l].astype(f32)
            for j in range(1, Y):
                total = total + pr[part, j - 1, l].astype(f32)
            ysum[part, l] = total.astype(bf16)
        return [
            wire.send(ysum.at[part, (me.l + j) % L], lr.at[part, j - 1], me.at_l(j))
            for j in range(1, L)
        ]

    select = selection(3)
    arrived(3, 0)
    p2[0] = gather_sum(3, 0, select).astype(bf16)
    far_up = wire.send(p2.at[0], fm, me.at_z(1))
    arrived(3, 1)
    spread(2, 1)
    spread(1, 0)
    p2[1] = gather_sum(3, 1, select).astype(bf16)
    far_down = wire.send(p2.at[1], fp, me.at_z(-1))

    for copy in g_a:
        copy.wait_recv()
    ga[pl.ds(me.p, 1)] = gsum[pl.ds(me.p, 1)]
    gmine[...] = jnp.sum(ga[...].astype(f32), axis=0).astype(bf16)
    g_b = [wire.send(gmine, gb.at[j - 1], me.at_z(j)) for j in range(1, Z)]

    select_up, select_down = selection(2), selection(1)
    arrived(2, 1)
    arrived(1, 0)
    spread(2, 0)
    spread(1, 1)
    p1[1] = gather_sum(2, 1, select_up).astype(bf16)
    v_up = wire.send(p1.at[1], rm.at[1], me.at_z(1))
    p3[0] = gather_sum(1, 0, select_down).astype(bf16)
    k_down = wire.send(p3.at[0], rp.at[0], me.at_z(-1))

    for copy in g_b:
        copy.wait_recv()
    gpiece[...] = (
        gmine[...].astype(f32) + jnp.sum(gb[...].astype(f32), axis=0)
    ).astype(bf16)
    gall[pl.ds(me.p, 1)] = gpiece[...][None]
    g_c = [wire.send(gpiece, gall.at[me.p], me.at_p(j)) for j in range(1, PN)]

    arrived(2, 0)
    arrived(1, 1)
    spread(0, 0)
    spread(0, 1)
    up = gather_sum(2, 0, select_up)
    down = gather_sum(1, 1, select_down)
    far_up.wait_recv()
    p1[0] = (up + fm[...].astype(f32)).astype(bf16)
    k_up = wire.send(p1.at[0], rm.at[0], me.at_z(1))
    far_down.wait_recv()
    p3[1] = (down + fp[...].astype(f32)).astype(bf16)
    v_down = wire.send(p3.at[1], rp.at[1], me.at_z(-1))
    l_sends = [y_stage(0)]

    select = selection(0)
    totals = []
    for part in range(2):
        arrived(0, part)
        totals.append(gather_sum(0, part, select) + own[part])
    l_sends.append(y_stage(1))
    for copy in edges + g_c:
        copy.wait_recv()
    everyone = gall[...].reshape(2, 2, BLOCK, HEAD_DIM).astype(f32)
    for part in range(2):
        ones = []
        for b in range(blocks):
            one = totals[part][b]
            for j in range(2):
                one = one + jnp.where(ghit[j] == b, everyone[j, part], 0.0)
            if b == 0:
                one = one + halo[0, part].astype(f32)
            if b == blocks - 1:
                one = one + halo[1, part].astype(f32)
            ones.append(one[None])
        totals[part] = jnp.concatenate(ones, axis=0)

    for part in range(2):
        for copy in l_sends[part]:
            copy.wait_recv()
        total = ysum[part, pl.ds(me.l, 1)][0].astype(f32)
        for j in range(1, L):
            total = total + lr[part, j - 1].astype(f32)
        out[part * half : (part + 1) * half] = total.astype(bf16)

    v_up.wait_recv()
    k_down.wait_recv()
    k_up.wait_recv()
    v_down.wait_recv()
    for part, target in ((0, dk), (1, dv)):
        total = totals[part] + (rm[part].astype(f32) + rp[part].astype(f32))
        target[...] = total.reshape(target.shape).astype(bf16)
    wire.finish()


def plan(dims, pattern, blocks):
    me = Place(dims)
    Z, PN, Y, L = dims
    seqs = Z * PN
    head = lax.dynamic_slice_in_dim(pattern, me.dp, 1, 0)[0]
    shared = head[0, :2]
    entries = 3 * blocks
    mine = lax.dynamic_slice_in_dim(head, me.z * PN * blocks, PN * blocks, 0)
    wanted = mine[:, 2:].reshape(PN, entries)
    owner = wanted // blocks
    e = jnp.arange(entries, dtype=jnp.int32)
    same = owner[:, :, None] == owner[:, None, :]
    rank = jnp.sum((same & (e[None, :] < e[:, None])).astype(jnp.int32), axis=-1)
    rel = jnp.array([0, Z - 1, 1, 2], jnp.int32)
    places = (me.z + rel) % Z
    c = jnp.arange(CAP, dtype=jnp.int32)
    column = places * PN + me.p
    hit = (owner[None, :, None, :] == column[:, None, None, None]) & (
        rank[None, :, None, :] == c[None, None, :, None]
    )
    pick = jnp.sum(jnp.where(hit, wanted[None, :, None, :] % blocks + 1, 0), axis=-1) - 1
    my_owner = lax.dynamic_slice_in_dim(owner, me.p, 1, 0)[0]
    my_rank = lax.dynamic_slice_in_dim(rank, me.p, 1, 0)[0]
    back = (my_owner // PN - me.z) % Z
    order_of = jnp.where(back == 0, 0, jnp.where(back == 1, 2, jnp.where(back == 2, 3, 1)))
    flat = (order_of * PN + my_owner % PN) * CAP + my_rank
    slots = jnp.arange(4 * PN * CAP, dtype=jnp.int32)
    entry_of = entries - jnp.sum(
        jnp.where(flat[None, :] == slots[:, None], entries - e[None, :], 0), axis=-1
    )
    slot_of = flat + order_of * (PN * CAP)
    g_seq = shared // blocks
    g_owner = jnp.concatenate([g_seq % PN, (me.z - g_seq // PN) % Z])
    ghit = jnp.where(g_seq == me.seq, shared % blocks, -1)
    return pick, slot_of, entry_of, shared % blocks, g_owner, ghit


def vmem():
    return pl.BlockSpec(memory_space=pltpu.VMEM)


def smem():
    return pl.BlockSpec(memory_space=pltpu.SMEM)


def per_device(dims, queries, keys, values, out_weight, grad_out, pattern):
    Z, PN, Y, L = dims
    tokens = queries.shape[0]
    blocks = tokens // BLOCK
    rows = out_weight.shape[0]
    piece = 4 * BLOCK // PN
    block = (BLOCK, HEAD_DIM)
    pair = (2,) + block
    half = tokens // 2
    shape = jax.ShapeDtypeStruct
    pick, slot_of, entry_of, g_pick, g_owner, ghit = plan(dims, pattern, blocks)

    gather_sems = 160
    halo, glob, rnd, wh, gctx = pl.pallas_call(
        functools.partial(gather_kernel, dims),
        out_shape=(
            shape((2,) + pair, bf16),
            shape((PN, piece, HEAD_DIM), bf16),
            shape((4, 2, PN, CAP) + block, bf16),
            shape((Y * L, HEAD_DIM, HEAD_DIM), bf16),
            shape((tokens, HEAD_DIM), bf16),
        ),
        in_specs=[vmem()] * 4 + [smem()] * 3,
        out_specs=(vmem(),) * 5,
        scratch_shapes=[
            *([pltpu.VMEM((blocks,) + block, bf16)] * 8),
            *([pltpu.VMEM((2, PN, CAP) + block, bf16)] * 4),
            pltpu.VMEM((2,) + pair, bf16),
            pltpu.VMEM((PN, piece, HEAD_DIM), bf16),
            pltpu.VMEM((PN, piece, HEAD_DIM), bf16),
            pltpu.VMEM((piece, HEAD_DIM), bf16),
            pltpu.VMEM((Z, piece, HEAD_DIM), bf16),
            pltpu.VMEM((piece, HEAD_DIM), bf16),
            pltpu.VMEM((rows, HEAD_DIM), bf16),
            pltpu.VMEM((Z, rows, HEAD_DIM), bf16),
            pltpu.VMEM((PN, Z, rows, HEAD_DIM), bf16),
            pltpu.VMEM((Y, L, tokens, HEAD_DIM), bf16),
            pltpu.SemaphoreType.DMA((gather_sems,)),
            pltpu.SemaphoreType.DMA((gather_sems,)),
        ],
        compiler_params=pltpu.CompilerParams(
            collective_id=0, has_side_effects=True, vmem_limit_bytes=VMEM_LIMIT
        ),
    )(keys, values, out_weight, grad_out, jnp.maximum(pick, 0).reshape(-1), g_pick, g_owner)

    slots = 4 * PN * CAP
    ctx, dq, sb, own, edge, gsum = pl.pallas_call(
        attend_kernel,
        out_shape=(
            shape((tokens, HEAD_DIM), bf16),
            shape((tokens, HEAD_DIM), bf16),
            shape((2 * slots,) + block, bf16),
            shape((2, blocks) + block, f32),
            shape((2,) + pair, bf16),
            shape((4,) + block, bf16),
        ),
        in_specs=[vmem()] * 7 + [smem()] * 2,
        out_specs=(vmem(),) * 6,
        scratch_shapes=[pltpu.VMEM((3 * blocks + 1,) + pair, bf16)],
        compiler_params=pltpu.CompilerParams(vmem_limit_bytes=VMEM_LIMIT),
    )(
        queries, keys, values, halo, glob.reshape((4,) + block),
        rnd.reshape((2 * slots,) + block), gctx, slot_of, entry_of,
    )

    scatter_sems = 160
    landing = pltpu.VMEM((2, PN, CAP) + block, bf16)
    half_sum = pltpu.VMEM((blocks,) + block, bf16)
    whole_sum = pltpu.VMEM((2, blocks) + block, bf16)
    out, dk, dv = pl.pallas_call(
        functools.partial(scatter_kernel, dims),
        out_shape=(shape((tokens, HEAD_DIM), bf16),) * 3,
        in_specs=[vmem()] * 7 + [smem()],
        out_specs=(vmem(),) * 3,
        scratch_shapes=[
            pltpu.VMEM((2,) + pair, bf16),
            landing, landing, landing, landing,
            whole_sum, whole_sum, whole_sum, half_sum, half_sum, whole_sum, whole_sum,
            pltpu.VMEM((PN, piece, HEAD_DIM), bf16),
            pltpu.VMEM((piece, HEAD_DIM), bf16),
            pltpu.VMEM((Z - 1, piece, HEAD_DIM), bf16),
            pltpu.VMEM((piece, HEAD_DIM), bf16),
            pltpu.VMEM((PN, piece, HEAD_DIM), bf16),
            pltpu.VMEM((2, Y, L, half, HEAD_DIM), bf16),
            pltpu.VMEM((2, max(Y - 1, 1), L, half, HEAD_DIM), bf16),
            pltpu.VMEM((2, L, half, HEAD_DIM), bf16),
            pltpu.VMEM((2, max(L - 1, 1), half, HEAD_DIM), bf16),
            pltpu.SemaphoreType.DMA((scatter_sems,)),
            pltpu.SemaphoreType.DMA((scatter_sems,)),
        ],
        compiler_params=pltpu.CompilerParams(
            collective_id=1, has_side_effects=True, vmem_limit_bytes=VMEM_LIMIT
        ),
    )(
        ctx, wh, sb.reshape((4, 2, PN, CAP) + block), own, edge,
        gsum.reshape(PN, piece, HEAD_DIM), jnp.repeat(pick.reshape(4, PN * CAP), 16, axis=1),
        ghit,
    )
    return out, dq, dk, dv


def solution(mesh, planes=8, lines=4):
    seq, dp = mesh.shape["seq"], mesh.shape["dp"]
    dims = (seq // planes, planes, dp // lines, lines)
    tile = P("seq", "dp")
    return jax.shard_map(
        functools.partial(per_device, dims),
        mesh=mesh,
        in_specs=(tile,) * 5 + (P(),),
        out_specs=(tile,) * 4,
        check_vma=False,
    )
```

time: 148 us -> 169 us (1.14)
  the two profiles are of different devices: /device:TPU:33 before, /device:TPU:41 now
where the time goes in v2:
time: 169 us
  Pallas kernels  159 us (94%)
  local copies, waits for them, and re-layouts  8.07 us (5%)
    pallas_call x1, Pallas kernels, per_device(): pl.pallas_call(functools.partial(gather_kernel, dims), out_shape=(shape((...  86.7 us
    pallas_call x1, Pallas kernels, per_device(): pl.pallas_call(functools.partial(scatter_kernel, dims), out_shape=(shape(...  65.2 us
    unnamed x17, local copies, waits for them, and re-layouts  7.14 us
    pallas_call x1, Pallas kernels, per_device(): pl.pallas_call(attend_kernel, out_shape=(shape((tokens, HEAD_DIM), bf16),...  6.72 us

profile of v2, /device:TPU:41, one launch (start us, length us, event | category | flops | bytes accessed | tf_op | source)
XLA Modules:
  0.0 168.9 jit_solution(415433852266663118)
XLA Ops:
  0.6 0.0 copy-start
  0.7 0.8 copy-done
  1.5 0.1 constant_dynamic-slice_fusion.3
  1.7 0.1 slice_reduce_fusion
  1.8 0.7 fusion.7
  2.5 0.1 copy.30
  2.6 0.1 reshape.183
  2.7 0.3 convert_reduce_fusion
  3.1 0.1 broadcast_compare_fusion
  3.2 0.2 select_reduce_fusion
  3.4 0.1 select_reduce_fusion.1
  3.5 0.1 copy.34
  3.6 0.1 copy.35
  3.7 0.1 copy.32
  3.8 0.1 max.12.pick
  3.9 0.1 broadcast_in_dim.58
  4.0 0.1 reshape.188.pickx
  4.1 0.0 copy-start.1
  4.1 0.9 copy-done.1
  5.0 0.0 copy-start.2
  5.0 0.9 copy-done.2
  5.9 0.0 copy-start.4
  5.9 0.9 copy-done.4
  6.8 0.0 copy-start.5
  6.8 0.7 copy-done.5
  7.5 86.7 %shard_map.102 = (bf16[2,2,64,128]{3,2,1,0:T(8,128)(2,1)S(1)}, bf16[8,32,128]{2,1,0:T(8,128)(2,1)S(1)}, bf16[4,2,8,2,64,128]{5,4,3,2,1,0:T(8,128)(2,1)S(1)}, bf1...) custom-call(bf16[512,128]{1,0:T(8,128)(2,1)S(1)} %copy-done.1, bf16[512,128]{1,0:T(8,128)(2,1)S(1)} %copy-done.2, ...), custom_call_target="tpu_custom_call" | custom-call | tf_op jit(solution)/shard_map/pallas_call | solution.py:540
  94.2 0.0 copy-start.3
  94.2 0.9 copy-done.3
  95.1 6.7 %shard_map.103 = (bf16[512,128]{1,0:T(8,128)(2,1)S(1)}, bf16[512,128]{1,0:T(8,128)(2,1)}, bf16[128,64,128]{2,1,0:T(8,128)(2,1)S(1)}, f32[2,8,64,128]{3,2,1,0:T(8...) custom-call(bf16[512,128]{1,0:T(8,128)(2,1)S(1)} %copy-done.3, ...), custom_call_target="tpu_custom_call" | custom-call | tf_op jit(solution)/shard_map/pallas_call | solution.py:573
  101.8 65.2 %shard_map.104 = (bf16[512,128]{1,0:T(8,128)(2,1)S(1)}, bf16[512,128]{1,0:T(8,128)(2,1)S(1)}, bf16[512,128]{1,0:T(8,128)(2,1)S(1)}) custom-call(bf16[512,128]{1,0:T(8,128)(2,1)S(1)} %get-tuple-element.22.ctx, bf16[16,128,128]{2,1,0:T(8,128)(2,1)S(1)} %get-tuple-element.23.wh, bf16[4,2,8,2,64,128]{5,4,3,2,1,0:T(8,128)(2,1)S(1)} %bitcast.31, ...), custom_call_target="tpu_custom_call" | custom-call | tf_op jit(solution)/shard_map/pallas_call | solution.py:596
  167.0 0.7 copy.48
  167.6 0.7 copy.49
  168.3 0.7 copy.50
  (14 shorter events, 0.2 us)
Async XLA Ops:
  0.6 0.9 copy-start
  4.1 0.9 copy-start.1
  5.0 0.9 copy-start.2
  5.9 0.9 copy-start.4
  6.8 0.7 copy-start.5
  94.2 0.9 copy-start.3

commit v3 on v1

v3 whole, which is shorter than its diff:
```python
import functools

import jax
import jax.numpy as jnp
from jax import lax
from jax.experimental import pallas as pl
from jax.experimental.pallas import tpu as pltpu
from jax.sharding import PartitionSpec as P

HEAD_DIM = 128
BLOCK = 64
SCALE = HEAD_DIM**-0.5
CAP = 2
PICK, WANT, ENTRY = 0, 32, 64
LANES = 128
VMEM_LIMIT = 48 * 1024 * 1024
MESH = pl.DeviceIdType.MESH
f32 = jnp.float32
bf16 = jnp.bfloat16


class Place:
    def __init__(self, dims):
        self.Z, self.P, self.Y, self.L = dims
        seq, dp = lax.axis_index("seq"), lax.axis_index("dp")
        self.seq, self.dp = seq, dp
        self.z, self.p = seq // self.P, seq % self.P
        self.y, self.l = dp // self.L, dp % self.L

    def at_z(self, j):
        return {"seq": (self.z + j) % self.Z * self.P + self.p, "dp": self.dp}

    def at_p(self, j):
        return {"seq": self.z * self.P + (self.p + j) % self.P, "dp": self.dp}

    def at_y(self, j):
        return {"seq": self.seq, "dp": (self.y + j) % self.Y * self.L + self.l}

    def at_l(self, j):
        return {"seq": self.seq, "dp": self.y * self.L + (self.l + j) % self.L}

    def at_s(self, j):
        return {"seq": (self.seq + j) % (self.Z * self.P), "dp": self.dp}

    def signal(self):
        partners = (
            [self.at_p(j) for j in range(1, self.P)]
            + [self.at_z(j) for j in range(1, self.Z)]
            + [self.at_y(j) for j in range(1, self.Y)]
            + [self.at_l(j) for j in range(1, self.L)]
            + [self.at_s(1), self.at_s(-1)]
        )
        barrier = pltpu.get_barrier_semaphore()
        for partner in partners:
            pl.semaphore_signal(barrier, inc=1, device_id=partner, device_id_type=MESH)
        return len(partners)

    def wait(self, count):
        pl.semaphore_wait(pltpu.get_barrier_semaphore(), count)


class Wire:
    def __init__(self, send_sems, recv_sems):
        self.send_sems, self.recv_sems = send_sems, recv_sems
        self.used = 0
        self.sent = []

    def send(self, src, dst, target):
        copy = pltpu.make_async_remote_copy(
            src_ref=src,
            dst_ref=dst,
            send_sem=self.send_sems.at[self.used],
            recv_sem=self.recv_sems.at[self.used],
            device_id=target,
            device_id_type=MESH,
        )
        self.used += 1
        copy.start()
        self.sent.append(copy)
        return copy

    def finish(self):
        for copy in self.sent:
            copy.wait_send()


def kernel(
    dims, q, k, v, w, go, wanted, shared,
    out, dq, dk, dv,
    qv, kblk, vblk, wv, gov, ivec, idx, edge,
    km, vm, kp, vp, k2, v2, sb0, sb1, sb2, sb3, rnd, halo, glob,
    gcand, ga, gmine, gb, gpiece, wcol, wall, ps, pr, ysum, lr, gctx,
    kcat, vcat, probs32, fr, ctx, own, sb, eout, gsum,
    ehalo, ar0, ar1, ar2, ar3, selects, p1, p2, p3, fm, fp, rm, rp,
    sa, smine, sg, spiece, sall, cr,
    send_sems, recv_sems, local_sems,
):
    me = Place(dims)
    Z, PN, Y, L = dims
    wire = Wire(send_sems, recv_sems)
    blocks = k.shape[0]
    entries = 3 * blocks
    half = go.shape[0] // 2
    piece = glob.shape[1]
    pieces = BLOCK // piece
    skip = PN * CAP

    local = [
        pltpu.make_async_copy(src, dst, local_sems.at[i])
        for i, (src, dst) in enumerate(((k, kblk), (v, vblk), (w, wv), (go, gov), (q, qv)))
    ]
    for copy in local:
        copy.start()
    partners = me.signal()

    want = wanted[...]
    lane = lax.broadcasted_iota(jnp.int32, want.shape, 1)
    owner = lax.shift_right_arithmetic(want, blocks.bit_length() - 1)
    rank = jnp.zeros_like(want)
    for e in range(entries):
        at = WANT + e
        rank = rank + jnp.where((owner == owner[:, at : at + 1]) & (lane > at), 1, 0)
    rank = jnp.minimum(rank, CAP - 1)
    listed = (lane >= WANT) & (lane < WANT + entries)
    table = jnp.zeros_like(want)
    for i, rel in enumerate((0, Z - 1, 1, 2)):
        column = (me.z + rel) % Z * PN + me.p
        for c in range(CAP):
            hit = listed & (owner == column) & (rank == c)
            found = jnp.where(hit, (want & (blocks - 1)) + 1, 0)
            found = jnp.minimum(jnp.sum(found, axis=1, keepdims=True), blocks) - 1
            table = jnp.where(lane == PICK + i * CAP + c, found, table)
    back = (lax.shift_right_arithmetic(owner, PN.bit_length() - 1) - me.z) & (Z - 1)
    order_of = jnp.where(back == 0, 0, jnp.where(back == 1, 2, jnp.where(back == 2, 3, 1)))
    flat = (order_of * PN + (owner & (PN - 1))) * CAP + rank
    table = jnp.where(listed, flat, table)
    slot_entry = jnp.full_like(want, entries)
    for e in range(entries):
        at = WANT + e
        slot_entry = jnp.where(lane - ENTRY == flat[:, at : at + 1], e, slot_entry)
    ivec[...] = jnp.where(lane >= ENTRY, slot_entry, table)
    to_scalars = pltpu.make_async_copy(ivec, idx, local_sems.at[5])
    to_scalars.start()

    for copy in local:
        copy.wait()
    edge[0, 0] = kblk[blocks - 1]
    edge[0, 1] = vblk[blocks - 1]
    edge[1, 0] = kblk[0]
    edge[1, 1] = vblk[0]
    g_seq = [shared[j] // blocks for j in range(2)]
    g_block = [shared[j] % blocks for j in range(2)]
    for j in range(2):
        for part, source in ((0, kblk), (1, vblk)):
            first = (j * 2 + part) * pieces
            gcand[first : first + pieces] = source[g_block[j]].reshape(pieces, piece, HEAD_DIM)
    to_scalars.wait()
    me.wait(partners)

    w_z = [wire.send(w, wcol.at[me.z], me.at_z(j)) for j in range(1, Z)]
    k_up = wire.send(k, km, me.at_z(1))
    k_down = wire.send(k, kp, me.at_z(-1))
    v_up = wire.send(v, vm, me.at_z(1))
    v_down = wire.send(v, vp, me.at_z(-1))
    g_a = [
        wire.send(gcand.at[(me.p + j) % PN], ga.at[me.p], me.at_p(j)) for j in range(1, PN)
    ]
    edges = [
        wire.send(edge.at[0], halo.at[0], me.at_s(1)),
        wire.send(edge.at[1], halo.at[1], me.at_s(-1)),
    ]
    arrivals = []

    def pack(at, part, source, buffer):
        for requester in range(PN):
            for c in range(CAP):
                block = jnp.maximum(idx[requester, PICK + at * CAP + c], 0)
                buffer[part, requester, c] = source(block)
        rnd[pl.ds((at * 2 + part) * skip + me.p * CAP, CAP)] = buffer[part, pl.ds(me.p, 1)][0]
        for j in range(1, PN):
            arrivals.append(
                wire.send(
                    buffer.at[part, (me.p + j) % PN],
                    rnd.at[pl.ds((at * 2 + part) * skip + me.p * CAP, CAP)],
                    me.at_p(j),
                )
            )

    pack(0, 0, lambda b: kblk[b], sb0)
    pack(0, 1, lambda b: vblk[b], sb0)

    wcol[pl.ds(me.z, 1)] = wv[...][None]
    for copy in w_z:
        copy.wait_recv()
    wall[:, pl.ds(me.p, 1)] = wcol[...][:, None]
    w_p = [wire.send(wcol, wall.at[:, me.p], me.at_p(j)) for j in range(1, PN)]

    ga[pl.ds(me.p, 1)] = gcand[pl.ds(me.p, 1)]
    for copy in g_a:
        copy.wait_recv()
    own_half = (me.p // (PN // 2)) % 2
    gmine[...] = ga[jnp.where(own_half == 0, g_seq[0] % PN, g_seq[1] % PN)]
    g_b = [wire.send(gmine, gb.at[j], me.at_z(j)) for j in range(1, Z)]

    row = lax.broadcasted_iota(jnp.int32, (16, blocks * 16), 0)
    col = lax.broadcasted_iota(jnp.int32, (16, blocks * 16), 1)
    diagonal = col % 16 == row
    for at in range(4):
        for slot in range(skip):
            block = idx[slot // CAP, PICK + at * CAP + slot % CAP]
            hit = diagonal & (col // 16 == block)
            selects[at, slot * 16 : (slot + 1) * 16] = jnp.where(hit, 1.0, 0.0).astype(bf16)

    for copy in w_p:
        copy.wait_recv()
    chunk_z = Z // Y
    width = L * HEAD_DIM
    y_sends = []
    for part in range(2):
        rows = gov[part * half : (part + 1) * half]
        for j in list(range(1, Y)) + [0]:
            to = (me.y + j) % Y
            weight = wall[pl.ds(to * chunk_z, chunk_z)].reshape(width, HEAD_DIM)
            terms = lax.dot_general(
                rows, weight, (((1,), (1,)), ((), ())), preferred_element_type=f32
            ).astype(bf16)
            for head in range(L):
                ps[part, j, head] = terms[:, head * HEAD_DIM : (head + 1) * HEAD_DIM]
            if j:
                y_sends.append(wire.send(ps.at[part, j], pr.at[part, j - 1], me.at_y(j)))

    low, high = pl.ds(0, blocks // 2), pl.ds(blocks // 2, blocks - blocks // 2)

    def forward(lower, upper, far):
        return [
            wire.send(lower.at[low], far.at[low], me.at_z(1)),
            wire.send(upper.at[high], far.at[high], me.at_z(-1)),
        ]

    def y_stage(part):
        for copy in y_sends[part * (Y - 1) : (part + 1) * (Y - 1)]:
            copy.wait_recv()
        for head in range(L):
            total = ps[part, 0, head].astype(f32)
            for j in range(1, Y):
                total = total + pr[part, j - 1, head].astype(f32)
            ysum[part, head] = total.astype(bf16)
        return [
            wire.send(ysum.at[part, (me.l + j) % L], lr.at[part, j - 1], me.at_l(j))
            for j in range(1, L)
        ]

    k_up.wait_recv()
    k_down.wait_recv()
    k_far = forward(km, kp, k2)
    pack(1, 0, lambda b: km[b], sb1)
    pack(2, 0, lambda b: kp[b], sb2)
    v_up.wait_recv()
    v_down.wait_recv()
    v_far = forward(vm, vp, v2)
    pack(1, 1, lambda b: vm[b], sb1)
    pack(2, 1, lambda b: vp[b], sb2)
    gb[0] = gmine[...]
    for copy in g_b:
        copy.wait_recv()
    g_rel = [(me.z - g_seq[j] // PN + Z) % Z for j in range(2)]
    gpiece[...] = gb[jnp.where(own_half == 0, g_rel[0], g_rel[1])]
    glob[pl.ds(me.p, 1)] = gpiece[...][None]
    g_c = [wire.send(gpiece, glob.at[me.p], me.at_p(j)) for j in range(1, PN)]
    for copy in k_far:
        copy.wait_recv()
    pack(3, 0, lambda b: k2[b], sb3)
    l_sends = [y_stage(0)]
    for copy in v_far:
        copy.wait_recv()
    pack(3, 1, lambda b: v2[b], sb3)
    l_sends.append(y_stage(1))
    for copy in edges + g_c + arrivals:
        copy.wait_recv()

    def window(b, part, source):
        before = halo[0, part] if b == 0 else source[b - 1]
        after = halo[1, part] if b == blocks - 1 else source[b + 1]
        return [before, source[b], after]

    def dot(a, b, dims):
        return lax.dot_general(a, b, (dims, ((), ())), preferred_element_type=f32)

    nt, nn, tn = ((1,), (1,)), ((1,), (0,)), ((0,), (0,))
    everyone = glob[...].reshape(2, 2, BLOCK, HEAD_DIM)
    span = [slice(b * BLOCK, (b + 1) * BLOCK) for b in range(blocks)]
    for b in range(blocks):
        slots = []
        for i in range(3):
            flat_slot = idx[me.p, WANT + b * 3 + i]
            slots.append(flat_slot + flat_slot // skip * skip)
        keys = jnp.concatenate(
            window(b, 0, kblk) + [everyone[0, 0], everyone[1, 0]] + [rnd[s] for s in slots],
            axis=0,
        )
        values = jnp.concatenate(
            window(b, 1, vblk) + [everyone[0, 1], everyone[1, 1]] + [rnd[s + skip] for s in slots],
            axis=0,
        )
        kcat[b] = keys
        vcat[b] = values
        scores = dot(qv[span[b]], keys, nt) * SCALE
        raised = jnp.exp(scores - jnp.max(scores, axis=-1, keepdims=True))
        probs = raised / jnp.sum(raised, axis=-1, keepdims=True)
        probs32[b] = probs
        ctx[span[b]] = dot(probs.astype(bf16), values, nn).astype(bf16)

    l_in = [wire.send(ctx, cr.at[me.y, me.l], me.at_l(j)) for j in range(1, L)]
    y_in = [wire.send(ctx, cr.at[me.y, me.l], me.at_y(j)) for j in range(1, Y)]
    cr[pl.ds(me.y, 1), pl.ds(me.l, 1)] = ctx[...][None, None]
    for part in range(2):
        for copy in l_sends[part]:
            copy.wait_recv()
        total = ysum[part, pl.ds(me.l, 1)][0].astype(f32)
        for j in range(1, L):
            total = total + lr[part, j - 1].astype(f32)
        gctx[part * half : (part + 1) * half] = total.astype(bf16)

    acc = {}
    total = [jnp.zeros((2 * BLOCK, HEAD_DIM), f32) for _ in range(2)]

    def settle(at):
        for part in range(2):
            term = acc.pop((at, part))
            if at < 0:
                eout[0, part] = term.astype(bf16)
            elif at >= blocks:
                eout[1, part] = term.astype(bf16)
            else:
                own[part, at] = term

    fr[entries] = jnp.zeros(fr.shape[1:], bf16)
    for b in range(blocks):
        qb, gb_rows = qv[span[b]], gctx[span[b]]
        probs = probs32[b]
        keys, values = kcat[b], vcat[b]
        delta = jnp.sum(
            gb_rows.astype(f32) * ctx[span[b]].astype(f32), axis=-1, keepdims=True
        )
        gscores = (probs * (dot(gb_rows, values, nt) - delta)).astype(bf16)
        dq[span[b]] = (dot(gscores, keys, nn) * SCALE).astype(bf16)
        for part, term in (
            (0, dot(gscores, qb, tn) * SCALE),
            (1, dot(probs.astype(bf16), gb_rows, tn)),
        ):
            for i in range(3):
                at = (b - 1 + i, part)
                one = term[i * BLOCK : (i + 1) * BLOCK]
                acc[at] = acc[at] + one if at in acc else one
            total[part] = total[part] + term[3 * BLOCK : 5 * BLOCK]
            for i in range(3):
                fr[b * 3 + i, part] = term[(5 + i) * BLOCK : (6 + i) * BLOCK].astype(bf16)
        settle(b - 1)
    settle(blocks - 1)
    settle(blocks)

    landing = (ar0, ar1, ar2, ar3)
    returned = {}

    def spread(at, part):
        for slot in range(skip):
            entry = idx[me.p, ENTRY + at * skip + slot]
            sb[at, part, slot // CAP, slot % CAP] = fr[entry, part]
        landing[at][part, pl.ds(me.p, 1)] = sb[at, part, pl.ds(me.p, 1)]
        returned[at, part] = [
            wire.send(sb.at[at, part, (me.p + j) % PN], landing[at].at[part, me.p], me.at_p(j))
            for j in range(1, PN)
        ]

    spread(3, 0)
    spread(3, 1)
    for j in range(2):
        for part in range(2):
            first = (j * 2 + part) * pieces
            gsum[first : first + pieces] = (
                total[part][j * BLOCK : (j + 1) * BLOCK]
                .astype(bf16)
                .reshape(pieces, piece, HEAD_DIM)
            )
    s_a = [
        wire.send(gsum.at[(me.p + j) % PN], sa.at[me.p], me.at_p(j)) for j in range(1, PN)
    ]
    edges = [
        wire.send(eout.at[0], ehalo.at[1], me.at_s(-1)),
        wire.send(eout.at[1], ehalo.at[0], me.at_s(1)),
    ]
    for at, part in ((1, 0), (2, 1), (1, 1), (2, 0), (0, 0), (0, 1)):
        spread(at, part)

    def gather_sum(at, part):
        for copy in returned[at, part]:
            copy.wait_recv()
        sums = []
        for r in range(BLOCK // 16):
            data = landing[at][part, :, :, r * 16 : (r + 1) * 16].reshape(skip * 16, HEAD_DIM)
            sums.append(dot(selects[at], data, tn).reshape(blocks, 16, HEAD_DIM))
        return jnp.concatenate(sums, axis=1)

    p2[0] = gather_sum(3, 0).astype(bf16)
    far_up = wire.send(p2.at[0], fm, me.at_z(1))
    p2[1] = gather_sum(3, 1).astype(bf16)
    far_down = wire.send(p2.at[1], fp, me.at_z(-1))

    for copy in s_a:
        copy.wait_recv()
    sa[pl.ds(me.p, 1)] = gsum[pl.ds(me.p, 1)]
    smine[...] = jnp.sum(sa[...].astype(f32), axis=0).astype(bf16)
    s_b = [wire.send(smine, sg.at[j - 1], me.at_z(j)) for j in range(1, Z)]

    p3[0] = gather_sum(1, 0).astype(bf16)
    k_down = wire.send(p3.at[0], rp.at[0], me.at_z(-1))
    p1[1] = gather_sum(2, 1).astype(bf16)
    v_up = wire.send(p1.at[1], rm.at[1], me.at_z(1))
    for j in range(1, L):
        l_in[j - 1].wait_recv()
        source = (me.l + L - j) % L
        for i in range(1, Y):
            y_in.append(wire.send(cr.at[me.y, source], cr.at[me.y, source], me.at_y(i)))
    down = gather_sum(1, 1)
    up = gather_sum(2, 0)
    far_up.wait_recv()
    p1[0] = (up + fm[...].astype(f32)).astype(bf16)
    k_up = wire.send(p1.at[0], rm.at[0], me.at_z(1))
    far_down.wait_recv()
    p3[1] = (down + fp[...].astype(f32)).astype(bf16)
    v_down = wire.send(p3.at[1], rp.at[1], me.at_z(-1))

    for copy in s_b:
        copy.wait_recv()
    spiece[...] = (
        smine[...].astype(f32) + jnp.sum(sg[...].astype(f32), axis=0)
    ).astype(bf16)
    sall[pl.ds(me.p, 1)] = spiece[...][None]
    s_c = [wire.send(spiece, sall.at[me.p], me.at_p(j)) for j in range(1, PN)]

    totals = [gather_sum(0, part) + own[part] for part in range(2)]
    for copy in y_in:
        copy.wait_recv()
    per_head = HEAD_DIM // w.shape[0]
    result = jnp.zeros(out.shape, f32)
    for y in range(Y):
        for l in range(L):
            head = y * L + l
            tiles = range(head * per_head, (head + 1) * per_head)
            weight = jnp.concatenate([wall[t // PN, t % PN] for t in tiles], axis=0)
            result = result + jnp.dot(cr[y, l], weight, preferred_element_type=f32)
    out[...] = result.astype(bf16)

    for copy in edges + s_c:
        copy.wait_recv()
    everyone = sall[...].reshape(2, 2, BLOCK, HEAD_DIM).astype(f32)
    g_here = [jnp.where(g_seq[j] == me.seq, g_block[j], -1) for j in range(2)]
    for part in range(2):
        ones = []
        for b in range(blocks):
            one = totals[part][b]
            for j in range(2):
                one = one + jnp.where(g_here[j] == b, everyone[j, part], 0.0)
            if b == 0:
                one = one + ehalo[0, part].astype(f32)
            if b == blocks - 1:
                one = one + ehalo[1, part].astype(f32)
            ones.append(one[None])
        totals[part] = jnp.concatenate(ones, axis=0)
    for copy in (v_up, k_down, k_up, v_down):
        copy.wait_recv()
    for part, target in ((0, dk), (1, dv)):
        total = totals[part] + (rm[part].astype(f32) + rp[part].astype(f32))
        target[...] = total.reshape(target.shape).astype(bf16)
    wire.finish()


def per_device(dims, queries, keys, values, out_weight, grad_out, pattern):
    Z, PN, Y, L = dims
    me = Place(dims)
    tokens = queries.shape[0]
    blocks = tokens // BLOCK
    entries = 3 * blocks
    rows = out_weight.shape[0]
    piece = 4 * BLOCK // PN
    half = tokens // 2
    block = (BLOCK, HEAD_DIM)
    any_space = pl.BlockSpec(memory_space=pl.ANY)
    in_vmem = pl.BlockSpec(memory_space=pltpu.VMEM)
    shape = jax.ShapeDtypeStruct

    plane = lax.dynamic_slice(
        pattern, (me.dp, me.z * PN * blocks, 0), (1, PN * blocks, pattern.shape[2])
    )[0]
    wanted = jnp.pad(
        plane[:, 2:].reshape(PN, entries),
        ((0, 0), (WANT, LANES - WANT - entries)),
        constant_values=-1,
    )

    def buffer(*dims, dtype=bf16):
        return pltpu.VMEM(dims, dtype)

    keyed = buffer(blocks, *block)
    slots = buffer(2, PN, CAP, *block)
    pairs = buffer(2, 2, *block)
    whole = buffer(2, blocks, *block)
    small = buffer(piece, HEAD_DIM)
    spread_small = buffer(PN, piece, HEAD_DIM)
    out, dq, dk, dv = pl.pallas_call(
        functools.partial(kernel, dims),
        out_shape=(shape((tokens, HEAD_DIM), bf16),) * 4,
        in_specs=[any_space] * 5 + [in_vmem, pl.BlockSpec(memory_space=pltpu.SMEM)],
        out_specs=(in_vmem,) * 4,
        scratch_shapes=[
            buffer(tokens, HEAD_DIM), keyed, keyed, buffer(rows, HEAD_DIM),
            buffer(tokens, HEAD_DIM), buffer(PN, LANES, dtype=jnp.int32),
            pltpu.SMEM((PN, LANES), jnp.int32), pairs,
            keyed, keyed, keyed, keyed, keyed, keyed, slots, slots, slots, slots,
            buffer(8 * PN * CAP, *block), pairs, spread_small,
            spread_small, spread_small, small, buffer(Z, piece, HEAD_DIM), small,
            buffer(Z, rows, HEAD_DIM), buffer(Z, PN, rows, HEAD_DIM),
            buffer(2, Y, L, half, HEAD_DIM), buffer(2, max(Y - 1, 1), L, half, HEAD_DIM),
            buffer(2, L, half, HEAD_DIM), buffer(2, max(L - 1, 1), half, HEAD_DIM),
            buffer(tokens, HEAD_DIM),
            buffer(blocks, 8 * BLOCK, HEAD_DIM), buffer(blocks, 8 * BLOCK, HEAD_DIM),
            buffer(blocks, BLOCK, 8 * BLOCK, dtype=f32), buffer(entries + 1, 2, *block),
            buffer(tokens, HEAD_DIM), buffer(2, blocks, *block, dtype=f32),
            buffer(4, 2, PN, CAP, *block), pairs, spread_small,
            pairs, slots, slots, slots, slots,
            buffer(4, PN * CAP * 16, blocks * 16),
            whole, whole, whole, keyed, keyed, whole, whole,
            spread_small, small, buffer(Z - 1, piece, HEAD_DIM), small, spread_small,
            buffer(Y, L, tokens, HEAD_DIM),
            pltpu.SemaphoreType.DMA((256,)),
            pltpu.SemaphoreType.DMA((256,)),
            pltpu.SemaphoreType.DMA((6,)),
        ],
        compiler_params=pltpu.CompilerParams(
            collective_id=0, has_side_effects=True, vmem_limit_bytes=VMEM_LIMIT
        ),
    )(
        queries, keys.reshape((blocks,) + block), values.reshape((blocks,) + block),
        out_weight, grad_out, wanted, plane[0, :2],
    )
    return out, dq, dk, dv


def solution(mesh, planes=8, lines=4):
    seq, dp = mesh.shape["seq"], mesh.shape["dp"]
    dims = (seq // planes, planes, dp // lines, lines)
    tile = P("seq", "dp")
    return jax.shard_map(
        functools.partial(per_device, dims),
        mesh=mesh,
        in_specs=(tile,) * 5 + (P(),),
        out_specs=(tile,) * 4,
        check_vma=False,
    )
```

time: 148 us -> 132 us (0.89)
  the two profiles are of different devices: /device:TPU:33 before, /device:TPU:120 now
where the time goes in v3:
time: 132 us
  Pallas kernels  124 us (94%)
  local copies, waits for them, and re-layouts  7.21 us (5%)
    pallas_call x1, Pallas kernels, per_device(): pl.pallas_call(functools.partial(kernel, dims), out_shape=(shape((tokens,...  124 us
    unnamed x17, local copies, waits for them, and re-layouts  6.76 us

profile of v3, /device:TPU:120, one launch (start us, length us, event | category | flops | bytes accessed | tf_op | source)
XLA Modules:
  0.0 131.5 jit_solution(4602857586861934064)
XLA Ops:
  0.6 0.0 copy-start
  0.6 0.0 copy-start.1
  0.7 0.8 copy-done
  1.5 0.1 constant_dynamic-slice_fusion
  1.6 0.1 slice_reduce_fusion.shared
  1.7 0.1 copy.13
  1.8 0.0 copy-start.5
  1.8 0.1 reshape.19
  1.9 0.1 pad.4.wanted
  2.0 0.0 copy-done.1
  2.0 0.6 copy-done.5
  2.6 0.0 copy-start.2
  2.6 0.9 copy-done.2
  3.5 0.0 copy-start.3
  3.5 0.9 copy-done.3
  4.4 0.0 copy-start.4
  4.4 0.9 copy-done.4
  5.3 123.6 %shard_map.93 = (bf16[512,128]{1,0:T(8,128)(2,1)S(1)}, bf16[512,128]{1,0:T(8,128)(2,1)S(1)}, bf16[512,128]{1,0:T(8,128)(2,1)S(1)}, bf16[512,128]{1,0:T(8,128)(2,1)S(1)}) custom-call(bf16[512,128]{1,0:T(8,128)(2,1)S(1)} %copy-done.1, bf16[8,64,128]{2,1,0:T(8,128)(2,1)S(1)} %bitcast.5, bf16[8,64,128]{2,1,0:T(8,128)(2,1)S(1)} %bitcast.6, ...), custom_call_target="tpu_custom_call" | custom-call | tf_op jit(solution)/shard_map/pallas_call | solution.py:510
  128.9 0.7 copy.21
  129.6 0.7 copy.22
  130.2 0.7 copy.23
  130.9 0.7 copy.24
  (2 shorter events, 0.0 us)
Async XLA Ops:
  0.6 0.9 copy-start
  0.6 1.3 %copy-start.1 = (bf16[512,128]{1,0:T(8,128)(2,1)S(1)}, bf16[512,128]{1,0:T(8,128)(2,1)}, u32[]{:S(2)}) copy-start(bf16[512,128]{1,0:T(8,128)(2,1)} %q.1) | copy-start | bytes 393220
  1.8 0.7 copy-start.5
  2.6 0.9 copy-start.2
  3.5 0.9 copy-start.3
  4.4 0.9 copy-start.4

commit v4 on v3

--- a/solution.py
+++ b/solution.py
@@ -13,7 +13,7 @@
 CAP = 2
 PICK, WANT, ENTRY = 0, 32, 64
 LANES = 128
-VMEM_LIMIT = 48 * 1024 * 1024
+VMEM_LIMIT = 64 * 1024 * 1024
 MESH = pl.DeviceIdType.MESH
 f32 = jnp.float32
 bf16 = jnp.bfloat16
@@ -42,13 +42,14 @@
     def at_s(self, j):
         return {"seq": (self.seq + j) % (self.Z * self.P), "dp": self.dp}
 
-    def signal(self):
+    def signal(self, extra=()):
         partners = (
             [self.at_p(j) for j in range(1, self.P)]
             + [self.at_z(j) for j in range(1, self.Z)]
             + [self.at_y(j) for j in range(1, self.Y)]
             + [self.at_l(j) for j in range(1, self.L)]
             + [self.at_s(1), self.at_s(-1)]
+            + list(extra)
         )
         barrier = pltpu.get_barrier_semaphore()
         for partner in partners:
@@ -84,12 +85,25 @@
             copy.wait_send()
 
 
+def weight_route(me, dims, rows):
+    seqs, heads = dims[0] * dims[1], dims[2] * dims[3]
+    per_head = HEAD_DIM // rows
+    shift = seqs // 2
+    target = {
+        "seq": (me.seq % per_head * heads + me.dp + shift) % seqs,
+        "dp": me.seq // per_head,
+    }
+    tile = (me.seq + shift) % seqs
+    source = {"seq": me.dp * per_head + tile // heads, "dp": tile % heads}
+    return target, source
+
+
 def kernel(
     dims, q, k, v, w, go, wanted, shared,
     out, dq, dk, dv,
     qv, kblk, vblk, wv, gov, ivec, idx, edge,
     km, vm, kp, vp, k2, v2, sb0, sb1, sb2, sb3, rnd, halo, glob,
-    gcand, ga, gmine, gb, gpiece, wcol, wall, ps, pr, ysum, lr, gctx,
+    gcand, ga, gmine, gb, gpiece, wcol, wall, wmine, wrcol, wrall, gog, gctx,
     kcat, vcat, probs32, fr, ctx, own, sb, eout, gsum,
     ehalo, ar0, ar1, ar2, ar3, selects, p1, p2, p3, fm, fp, rm, rp,
     sa, smine, sg, spiece, sall, cr,
@@ -100,7 +114,6 @@
     wire = Wire(send_sems, recv_sems)
     blocks = k.shape[0]
     entries = 3 * blocks
-    half = go.shape[0] // 2
     piece = glob.shape[1]
     pieces = BLOCK // piece
     skip = PN * CAP
@@ -111,7 +124,8 @@
     ]
     for copy in local:
         copy.start()
-    partners = me.signal()
+    w_target, w_source = weight_route(me, dims, w.shape[0])
+    partners = me.signal([w_source])
 
     want = wanted[...]
     lane = lax.broadcasted_iota(jnp.int32, want.shape, 1)
@@ -157,11 +171,8 @@
     to_scalars.wait()
     me.wait(partners)
 
+    w_in = wire.send(w, wmine, w_target)
     w_z = [wire.send(w, wcol.at[me.z], me.at_z(j)) for j in range(1, Z)]
-    k_up = wire.send(k, km, me.at_z(1))
-    k_down = wire.send(k, kp, me.at_z(-1))
-    v_up = wire.send(v, vm, me.at_z(1))
-    v_down = wire.send(v, vp, me.at_z(-1))
     g_a = [
         wire.send(gcand.at[(me.p + j) % PN], ga.at[me.p], me.at_p(j)) for j in range(1, PN)
     ]
@@ -169,6 +180,11 @@
         wire.send(edge.at[0], halo.at[0], me.at_s(1)),
         wire.send(edge.at[1], halo.at[1], me.at_s(-1)),
     ]
+    k_up = wire.send(k, km, me.at_z(1))
+    k_down = wire.send(k, kp, me.at_z(-1))
+    v_up = wire.send(v, vm, me.at_z(1))
+    v_down = wire.send(v, vp, me.at_z(-1))
+    go_y = [wire.send(go, gog.at[me.y, me.l], me.at_y(j)) for j in range(1, Y)]
     arrivals = []
 
     def pack(at, part, source, buffer):
@@ -189,11 +205,12 @@
     pack(0, 0, lambda b: kblk[b], sb0)
     pack(0, 1, lambda b: vblk[b], sb0)
 
+    go_l = [wire.send(go, gog.at[me.y, me.l], me.at_l(j)) for j in range(1, L)]
+    gog[pl.ds(me.y, 1), pl.ds(me.l, 1)] = gov[...][None, None]
     wcol[pl.ds(me.z, 1)] = wv[...][None]
-    for copy in w_z:
-        copy.wait_recv()
-    wall[:, pl.ds(me.p, 1)] = wcol[...][:, None]
-    w_p = [wire.send(wcol, wall.at[:, me.p], me.at_p(j)) for j in range(1, PN)]
+    w_in.wait_recv()
+    wr_z = [wire.send(wmine, wrcol.at[me.z], me.at_z(j)) for j in range(1, Z)]
+    wrcol[pl.ds(me.z, 1)] = wmine[...][None]
 
     ga[pl.ds(me.p, 1)] = gcand[pl.ds(me.p, 1)]
     for copy in g_a:
@@ -211,24 +228,6 @@
             hit = diagonal & (col // 16 == block)
             selects[at, slot * 16 : (slot + 1) * 16] = jnp.where(hit, 1.0, 0.0).astype(bf16)
 
-    for copy in w_p:
-        copy.wait_recv()
-    chunk_z = Z // Y
-    width = L * HEAD_DIM
-    y_sends = []
-    for part in range(2):
-        rows = gov[part * half : (part + 1) * half]
-        for j in list(range(1, Y)) + [0]:
-            to = (me.y + j) % Y
-            weight = wall[pl.ds(to * chunk_z, chunk_z)].reshape(width, HEAD_DIM)
-            terms = lax.dot_general(
-                rows, weight, (((1,), (1,)), ((), ())), preferred_element_type=f32
-            ).astype(bf16)
-            for head in range(L):
-                ps[part, j, head] = terms[:, head * HEAD_DIM : (head + 1) * HEAD_DIM]
-            if j:
-                y_sends.append(wire.send(ps.at[part, j], pr.at[part, j - 1], me.at_y(j)))
-
     low, high = pl.ds(0, blocks // 2), pl.ds(blocks // 2, blocks - blocks // 2)
 
     def forward(lower, upper, far):
@@ -237,29 +236,25 @@
             wire.send(upper.at[high], far.at[high], me.at_z(-1)),
         ]
 
-    def y_stage(part):
-        for copy in y_sends[part * (Y - 1) : (part + 1) * (Y - 1)]:
-            copy.wait_recv()
-        for head in range(L):
-            total = ps[part, 0, head].astype(f32)
-            for j in range(1, Y):
-                total = total + pr[part, j - 1, head].astype(f32)
-            ysum[part, head] = total.astype(bf16)
-        return [
-            wire.send(ysum.at[part, (me.l + j) % L], lr.at[part, j - 1], me.at_l(j))
-            for j in range(1, L)
-        ]
-
     k_up.wait_recv()
     k_down.wait_recv()
     k_far = forward(km, kp, k2)
     pack(1, 0, lambda b: km[b], sb1)
     pack(2, 0, lambda b: kp[b], sb2)
+    for copy in wr_z:
+        copy.wait_recv()
+    wrall[pl.ds(me.p, 1)] = wrcol[...][None]
+    wr_p = [wire.send(wrcol, wrall.at[me.p], me.at_p(j)) for j in range(1, PN)]
     v_up.wait_recv()
     v_down.wait_recv()
     v_far = forward(vm, vp, v2)
     pack(1, 1, lambda b: vm[b], sb1)
     pack(2, 1, lambda b: vp[b], sb2)
+    for j in range(1, L):
+        go_l[j - 1].wait_recv()
+        source = (me.l + L - j) % L
+        for i in range(1, Y):
+            go_y.append(wire.send(gog.at[me.y, source], gog.at[me.y, source], me.at_y(i)))
     gb[0] = gmine[...]
     for copy in g_b:
         copy.wait_recv()
@@ -270,11 +265,12 @@
     for copy in k_far:
         copy.wait_recv()
     pack(3, 0, lambda b: k2[b], sb3)
-    l_sends = [y_stage(0)]
     for copy in v_far:
         copy.wait_recv()
     pack(3, 1, lambda b: v2[b], sb3)
-    l_sends.append(y_stage(1))
+    for copy in w_z:
+        copy.wait_recv()
+    wall[:, pl.ds(me.p, 1)] = wcol[...][:, None]
     for copy in edges + g_c + arrivals:
         copy.wait_recv()
 
@@ -313,13 +309,15 @@
     l_in = [wire.send(ctx, cr.at[me.y, me.l], me.at_l(j)) for j in range(1, L)]
     y_in = [wire.send(ctx, cr.at[me.y, me.l], me.at_y(j)) for j in range(1, Y)]
     cr[pl.ds(me.y, 1), pl.ds(me.l, 1)] = ctx[...][None, None]
-    for part in range(2):
-        for copy in l_sends[part]:
-            copy.wait_recv()
-        total = ysum[part, pl.ds(me.l, 1)][0].astype(f32)
-        for j in range(1, L):
-            total = total + lr[part, j - 1].astype(f32)
-        gctx[part * half : (part + 1) * half] = total.astype(bf16)
+    w_p = [wire.send(wcol, wall.at[:, me.p], me.at_p(j)) for j in range(1, PN)]
+    for copy in go_y + wr_p:
+        copy.wait_recv()
+    columns = []
+    for d in range(Y * L):
+        slots = [(i * Y * L + d + Z * PN // 2) % (Z * PN) for i in range(HEAD_DIM // w.shape[0])]
+        columns.append(jnp.concatenate([wrall[t % PN, t // PN] for t in slots], axis=0))
+    full = jnp.concatenate([gog[d // L, d % L] for d in range(Y * L)], axis=1)
+    gctx[...] = dot(full, jnp.concatenate(columns, axis=1), nt).astype(bf16)
 
     acc = {}
     total = [jnp.zeros((2 * BLOCK, HEAD_DIM), f32) for _ in range(2)]
@@ -439,17 +437,10 @@
     s_c = [wire.send(spiece, sall.at[me.p], me.at_p(j)) for j in range(1, PN)]
 
     totals = [gather_sum(0, part) + own[part] for part in range(2)]
-    for copy in y_in:
-        copy.wait_recv()
-    per_head = HEAD_DIM // w.shape[0]
-    result = jnp.zeros(out.shape, f32)
-    for y in range(Y):
-        for l in range(L):
-            head = y * L + l
-            tiles = range(head * per_head, (head + 1) * per_head)
-            weight = jnp.concatenate([wall[t // PN, t % PN] for t in tiles], axis=0)
-            result = result + jnp.dot(cr[y, l], weight, preferred_element_type=f32)
-    out[...] = result.astype(bf16)
+    for copy in y_in + w_p:
+        copy.wait_recv()
+    full = jnp.concatenate([cr[d // L, d % L] for d in range(Y * L)], axis=1)
+    out[...] = dot(full, wall[...].reshape(-1, HEAD_DIM), nn).astype(bf16)
 
     for copy in edges + s_c:
         copy.wait_recv()
@@ -475,6 +466,11 @@
     wire.finish()
 
 
+def settle_kernel(*refs):
+    for source, target in zip(refs[:4], refs[4:]):
+        target[...] = source[...]
+
+
 def per_device(dims, queries, keys, values, out_weight, grad_out, pattern):
     Z, PN, Y, L = dims
     me = Place(dims)
@@ -483,9 +479,8 @@
     entries = 3 * blocks
     rows = out_weight.shape[0]
     piece = 4 * BLOCK // PN
-    half = tokens // 2
     block = (BLOCK, HEAD_DIM)
-    any_space = pl.BlockSpec(memory_space=pl.ANY)
+    in_hbm = pl.BlockSpec(memory_space=pltpu.HBM)
     in_vmem = pl.BlockSpec(memory_space=pltpu.VMEM)
     shape = jax.ShapeDtypeStruct
 
@@ -510,7 +505,7 @@
     out, dq, dk, dv = pl.pallas_call(
         functools.partial(kernel, dims),
         out_shape=(shape((tokens, HEAD_DIM), bf16),) * 4,
-        in_specs=[any_space] * 5 + [in_vmem, pl.BlockSpec(memory_space=pltpu.SMEM)],
+        in_specs=[in_hbm] * 5 + [in_vmem, pl.BlockSpec(memory_space=pltpu.SMEM)],
         out_specs=(in_vmem,) * 4,
         scratch_shapes=[
             buffer(tokens, HEAD_DIM), keyed, keyed, buffer(rows, HEAD_DIM),
@@ -520,8 +515,8 @@
             buffer(8 * PN * CAP, *block), pairs, spread_small,
             spread_small, spread_small, small, buffer(Z, piece, HEAD_DIM), small,
             buffer(Z, rows, HEAD_DIM), buffer(Z, PN, rows, HEAD_DIM),
-            buffer(2, Y, L, half, HEAD_DIM), buffer(2, max(Y - 1, 1), L, half, HEAD_DIM),
-            buffer(2, L, half, HEAD_DIM), buffer(2, max(L - 1, 1), half, HEAD_DIM),
+            buffer(rows, HEAD_DIM), buffer(Z, rows, HEAD_DIM), buffer(PN, Z, rows, HEAD_DIM),
+            buffer(Y, L, tokens, HEAD_DIM),
             buffer(tokens, HEAD_DIM),
             buffer(blocks, 8 * BLOCK, HEAD_DIM), buffer(blocks, 8 * BLOCK, HEAD_DIM),
             buffer(blocks, BLOCK, 8 * BLOCK, dtype=f32), buffer(entries + 1, 2, *block),
@@ -543,7 +538,13 @@
         queries, keys.reshape((blocks,) + block), values.reshape((blocks,) + block),
         out_weight, grad_out, wanted, plane[0, :2],
     )
-    return out, dq, dk, dv
+    return pl.pallas_call(
+        settle_kernel,
+        out_shape=(shape((tokens, HEAD_DIM), bf16),) * 4,
+        in_specs=[in_vmem] * 4,
+        out_specs=(in_vmem,) * 4,
+        compiler_params=pltpu.CompilerParams(vmem_limit_bytes=VMEM_LIMIT),
+    )(out, dq, dk, dv)
 
 
 def solution(mesh, planes=8, lines=4):

time: 132 us -> 151 us (1.14)
  the two profiles are of different devices: /device:TPU:120 before, /device:TPU:57 now
where the time goes in v4:
time: 151 us
  Pallas kernels  148 us (98%)
  local copies, waits for them, and re-layouts  2.29 us (2%)
    pallas_call x1, Pallas kernels, per_device(): pl.pallas_call(functools.partial(kernel, dims), out_shape=(shape((tokens,...  146 us

profile of v4, /device:TPU:57, one launch (start us, length us, event | category | flops | bytes accessed | tf_op | source)
XLA Modules:
  0.0 150.8 jit_solution(9452810018120549296)
XLA Ops:
  0.7 0.8 constant_dynamic-slice_fusion
  1.5 0.6 slice_reduce_fusion.shared
  2.1 0.1 copy.13
  2.2 0.1 reshape.19
  2.3 0.7 pad.4.wanted
  2.9 146.0 %shard_map.93 = (bf16[512,128]{1,0:T(8,128)(2,1)}, bf16[512,128]{1,0:T(8,128)(2,1)}, bf16[512,128]{1,0:T(8,128)(2,1)}, bf16[512,128]{1,0:T(8,128)(2,1)}) custom-call(bf16[512,128]{1,0:T(8,128)(2,1)} %q.1, bf16[8,64,128]{2,1,0:T(8,128)(2,1)} %bitcast.5, bf16[8,64,128]{2,1,0:T(8,128)(2,1)} %bitcast.6, bf16[64,128]{1,0:T(8,128)(2,1)} %w.1, ...), custom_call_target="tpu_custom_call" | custom-call | tf_op jit(solution)/shard_map/pallas_call | solution.py:505
  148.9 1.9 %shard_map.94 = (bf16[512,128]{1,0:T(8,128)(2,1)}, bf16[512,128]{1,0:T(8,128)(2,1)}, bf16[512,128]{1,0:T(8,128)(2,1)}, bf16[512,128]{1,0:T(8,128)(2,1)}) custom-call(bf16[512,128]{1,0:T(8,128)(2,1)} %get-tuple-element.8.refs_0_, bf16[512,128]{1,0:T(8,128)(2,1)} %get-tuple-element.9.refs_1_, bf16[512,128]{1,0:T(8,128)(2,1)} %get-tuple-element.10.refs_2_, ...), custom_call_target="tpu_custom_call" | custom-call | tf_op jit(solution)/shard_map/pallas_call | solution.py:541
  (2 shorter events, 0.0 us)

commit v5 on v3

--- a/solution.py
+++ b/solution.py
@@ -13,7 +13,7 @@
 CAP = 2
 PICK, WANT, ENTRY = 0, 32, 64
 LANES = 128
-VMEM_LIMIT = 48 * 1024 * 1024
+VMEM_LIMIT = 64 * 1024 * 1024
 MESH = pl.DeviceIdType.MESH
 f32 = jnp.float32
 bf16 = jnp.bfloat16
@@ -158,10 +158,6 @@
     me.wait(partners)
 
     w_z = [wire.send(w, wcol.at[me.z], me.at_z(j)) for j in range(1, Z)]
-    k_up = wire.send(k, km, me.at_z(1))
-    k_down = wire.send(k, kp, me.at_z(-1))
-    v_up = wire.send(v, vm, me.at_z(1))
-    v_down = wire.send(v, vp, me.at_z(-1))
     g_a = [
         wire.send(gcand.at[(me.p + j) % PN], ga.at[me.p], me.at_p(j)) for j in range(1, PN)
     ]
@@ -169,6 +165,10 @@
         wire.send(edge.at[0], halo.at[0], me.at_s(1)),
         wire.send(edge.at[1], halo.at[1], me.at_s(-1)),
     ]
+    k_up = wire.send(k, km, me.at_z(1))
+    k_down = wire.send(k, kp, me.at_z(-1))
+    v_up = wire.send(v, vm, me.at_z(1))
+    v_down = wire.send(v, vp, me.at_z(-1))
     arrivals = []
 
     def pack(at, part, source, buffer):
@@ -186,14 +186,15 @@
                 )
             )
 
+
+    wcol[pl.ds(me.z, 1)] = wv[...][None]
+    for copy in w_z:
+        copy.wait_recv()
+    wall[:, pl.ds(me.p, 1)] = wcol[...][:, None]
+    w_p = [wire.send(wcol, wall.at[:, me.p], me.at_p(j)) for j in range(1, PN)]
+
     pack(0, 0, lambda b: kblk[b], sb0)
     pack(0, 1, lambda b: vblk[b], sb0)
-
-    wcol[pl.ds(me.z, 1)] = wv[...][None]
-    for copy in w_z:
-        copy.wait_recv()
-    wall[:, pl.ds(me.p, 1)] = wcol[...][:, None]
-    w_p = [wire.send(wcol, wall.at[:, me.p], me.at_p(j)) for j in range(1, PN)]
 
     ga[pl.ds(me.p, 1)] = gcand[pl.ds(me.p, 1)]
     for copy in g_a:
@@ -441,15 +442,8 @@
     totals = [gather_sum(0, part) + own[part] for part in range(2)]
     for copy in y_in:
         copy.wait_recv()
-    per_head = HEAD_DIM // w.shape[0]
-    result = jnp.zeros(out.shape, f32)
-    for y in range(Y):
-        for l in range(L):
-            head = y * L + l
-            tiles = range(head * per_head, (head + 1) * per_head)
-            weight = jnp.concatenate([wall[t // PN, t % PN] for t in tiles], axis=0)
-            result = result + jnp.dot(cr[y, l], weight, preferred_element_type=f32)
-    out[...] = result.astype(bf16)
+    full = jnp.concatenate([cr[d // L, d % L] for d in range(Y * L)], axis=1)
+    out[...] = dot(full, wall[...].reshape(-1, HEAD_DIM), nn).astype(bf16)
 
     for copy in edges + s_c:
         copy.wait_recv()
@@ -475,6 +469,11 @@
     wire.finish()
 
 
+def settle_kernel(*refs):
+    for source, target in zip(refs[:4], refs[4:]):
+        target[...] = source[...]
+
+
 def per_device(dims, queries, keys, values, out_weight, grad_out, pattern):
     Z, PN, Y, L = dims
     me = Place(dims)
@@ -485,7 +484,7 @@
     piece = 4 * BLOCK // PN
     half = tokens // 2
     block = (BLOCK, HEAD_DIM)
-    any_space = pl.BlockSpec(memory_space=pl.ANY)
+    in_hbm = pl.BlockSpec(memory_space=pltpu.HBM)
     in_vmem = pl.BlockSpec(memory_space=pltpu.VMEM)
     shape = jax.ShapeDtypeStruct
 
@@ -510,7 +509,7 @@
     out, dq, dk, dv = pl.pallas_call(
         functools.partial(kernel, dims),
         out_shape=(shape((tokens, HEAD_DIM), bf16),) * 4,
-        in_specs=[any_space] * 5 + [in_vmem, pl.BlockSpec(memory_space=pltpu.SMEM)],
+        in_specs=[in_hbm] * 5 + [in_vmem, pl.BlockSpec(memory_space=pltpu.SMEM)],
         out_specs=(in_vmem,) * 4,
         scratch_shapes=[
             buffer(tokens, HEAD_DIM), keyed, keyed, buffer(rows, HEAD_DIM),
@@ -543,7 +542,13 @@
         queries, keys.reshape((blocks,) + block), values.reshape((blocks,) + block),
         out_weight, grad_out, wanted, plane[0, :2],
     )
-    return out, dq, dk, dv
+    return pl.pallas_call(
+        settle_kernel,
+        out_shape=(shape((tokens, HEAD_DIM), bf16),) * 4,
+        in_specs=[in_vmem] * 4,
+        out_specs=(in_vmem,) * 4,
+        compiler_params=pltpu.CompilerParams(vmem_limit_bytes=VMEM_LIMIT),
+    )(out, dq, dk, dv)
 
 
 def solution(mesh, planes=8, lines=4):

time: 132 us -> 130 us (0.985)
  the two profiles are of different devices: /device:TPU:120 before, /device:TPU:89 now
where the time goes in v5:
time: 130 us
  Pallas kernels  127 us (98%)
  local copies, waits for them, and re-layouts  2.29 us (2%)
    pallas_call x1, Pallas kernels, per_device(): pl.pallas_call(functools.partial(kernel, dims), out_shape=(shape((tokens,...  125 us

profile of v5, /device:TPU:89, one launch (start us, length us, event | category | flops | bytes accessed | tf_op | source)
XLA Modules:
  0.0 130.0 jit_solution(5907621468239171068)
XLA Ops:
  0.7 0.8 constant_dynamic-slice_fusion
  1.5 0.6 slice_reduce_fusion.shared
  2.1 0.1 copy.13
  2.2 0.1 reshape.19
  2.3 0.7 pad.4.wanted
  2.9 125.2 %shard_map.93 = (bf16[512,128]{1,0:T(8,128)(2,1)}, bf16[512,128]{1,0:T(8,128)(2,1)}, bf16[512,128]{1,0:T(8,128)(2,1)}, bf16[512,128]{1,0:T(8,128)(2,1)}) custom-call(bf16[512,128]{1,0:T(8,128)(2,1)} %q.1, bf16[8,64,128]{2,1,0:T(8,128)(2,1)} %bitcast.5, bf16[8,64,128]{2,1,0:T(8,128)(2,1)} %bitcast.6, bf16[64,128]{1,0:T(8,128)(2,1)} %w.1, ...), custom_call_target="tpu_custom_call" | custom-call | tf_op jit(solution)/shard_map/pallas_call | solution.py:509
  128.1 1.9 %shard_map.94 = (bf16[512,128]{1,0:T(8,128)(2,1)}, bf16[512,128]{1,0:T(8,128)(2,1)}, bf16[512,128]{1,0:T(8,128)(2,1)}, bf16[512,128]{1,0:T(8,128)(2,1)}) custom-call(bf16[512,128]{1,0:T(8,128)(2,1)} %get-tuple-element.8.refs_0_, bf16[512,128]{1,0:T(8,128)(2,1)} %get-tuple-element.9.refs_1_, bf16[512,128]{1,0:T(8,128)(2,1)} %get-tuple-element.10.refs_2_, ...), custom_call_target="tpu_custom_call" | custom-call | tf_op jit(solution)/shard_map/pallas_call | solution.py:545
  (2 shorter events, 0.0 us)

commit v6 on v5

--- a/solution.py
+++ b/solution.py
@@ -11,6 +11,7 @@
 BLOCK = 64
 SCALE = HEAD_DIM**-0.5
 CAP = 2
+QUARTERS = 4
 PICK, WANT, ENTRY = 0, 32, 64
 LANES = 128
 VMEM_LIMIT = 64 * 1024 * 1024
@@ -100,7 +101,7 @@
     wire = Wire(send_sems, recv_sems)
     blocks = k.shape[0]
     entries = 3 * blocks
-    half = go.shape[0] // 2
+    half = go.shape[0] // QUARTERS
     piece = glob.shape[1]
     pieces = BLOCK // piece
     skip = PN * CAP
@@ -217,7 +218,7 @@
     chunk_z = Z // Y
     width = L * HEAD_DIM
     y_sends = []
-    for part in range(2):
+    for part in range(QUARTERS):
         rows = gov[part * half : (part + 1) * half]
         for j in list(range(1, Y)) + [0]:
             to = (me.y + j) % Y
@@ -271,11 +272,11 @@
     for copy in k_far:
         copy.wait_recv()
     pack(3, 0, lambda b: k2[b], sb3)
-    l_sends = [y_stage(0)]
+    l_sends = [y_stage(0), y_stage(1)]
     for copy in v_far:
         copy.wait_recv()
     pack(3, 1, lambda b: v2[b], sb3)
-    l_sends.append(y_stage(1))
+    l_sends += [y_stage(2), y_stage(3)]
     for copy in edges + g_c + arrivals:
         copy.wait_recv()
 
@@ -314,7 +315,7 @@
     l_in = [wire.send(ctx, cr.at[me.y, me.l], me.at_l(j)) for j in range(1, L)]
     y_in = [wire.send(ctx, cr.at[me.y, me.l], me.at_y(j)) for j in range(1, Y)]
     cr[pl.ds(me.y, 1), pl.ds(me.l, 1)] = ctx[...][None, None]
-    for part in range(2):
+    for part in range(QUARTERS):
         for copy in l_sends[part]:
             copy.wait_recv()
         total = ysum[part, pl.ds(me.l, 1)][0].astype(f32)
@@ -482,7 +483,7 @@
     entries = 3 * blocks
     rows = out_weight.shape[0]
     piece = 4 * BLOCK // PN
-    half = tokens // 2
+    half = tokens // QUARTERS
     block = (BLOCK, HEAD_DIM)
     in_hbm = pl.BlockSpec(memory_space=pltpu.HBM)
     in_vmem = pl.BlockSpec(memory_space=pltpu.VMEM)
@@ -519,8 +520,8 @@
             buffer(8 * PN * CAP, *block), pairs, spread_small,
             spread_small, spread_small, small, buffer(Z, piece, HEAD_DIM), small,
             buffer(Z, rows, HEAD_DIM), buffer(Z, PN, rows, HEAD_DIM),
-            buffer(2, Y, L, half, HEAD_DIM), buffer(2, max(Y - 1, 1), L, half, HEAD_DIM),
-            buffer(2, L, half, HEAD_DIM), buffer(2, max(L - 1, 1), half, HEAD_DIM),
+            buffer(QUARTERS, Y, L, half, HEAD_DIM), buffer(QUARTERS, max(Y - 1, 1), L, half, HEAD_DIM),
+            buffer(QUARTERS, L, half, HEAD_DIM), buffer(QUARTERS, max(L - 1, 1), half, HEAD_DIM),
             buffer(tokens, HEAD_DIM),
             buffer(blocks, 8 * BLOCK, HEAD_DIM), buffer(blocks, 8 * BLOCK, HEAD_DIM),
             buffer(blocks, BLOCK, 8 * BLOCK, dtype=f32), buffer(entries + 1, 2, *block),

time: 130 us -> 132 us (1.015)
  the two profiles are of different devices: /device:TPU:89 before, /device:TPU:120 now
where the time goes in v6:
time: 132 us; the launch traced here: 131 us
  Pallas kernels  128 us (97%)
  local copies, waits for them, and re-layouts  2.29 us (2%)
    pallas_call x1, Pallas kernels, per_device(): pl.pallas_call(functools.partial(kernel, dims), out_shape=(shape((tokens,...  127 us

profile of v6, /device:TPU:120, one launch (start us, length us, event | category | flops | bytes accessed | tf_op | source)
XLA Modules:
  0.0 131.3 jit_solution(14600340335903365641)
XLA Ops:
  0.7 0.8 constant_dynamic-slice_fusion
  1.5 0.6 slice_reduce_fusion.shared
  2.1 0.1 copy.13
  2.2 0.1 reshape.19
  2.3 0.7 pad.4.wanted
  2.9 126.5 %shard_map.93 = (bf16[512,128]{1,0:T(8,128)(2,1)}, bf16[512,128]{1,0:T(8,128)(2,1)}, bf16[512,128]{1,0:T(8,128)(2,1)}, bf16[512,128]{1,0:T(8,128)(2,1)}) custom-call(bf16[512,128]{1,0:T(8,128)(2,1)} %q.1, bf16[8,64,128]{2,1,0:T(8,128)(2,1)} %bitcast.5, bf16[8,64,128]{2,1,0:T(8,128)(2,1)} %bitcast.6, bf16[64,128]{1,0:T(8,128)(2,1)} %w.1, ...), custom_call_target="tpu_custom_call" | custom-call | tf_op jit(solution)/shard_map/pallas_call | solution.py:510
  129.5 1.9 %shard_map.94 = (bf16[512,128]{1,0:T(8,128)(2,1)}, bf16[512,128]{1,0:T(8,128)(2,1)}, bf16[512,128]{1,0:T(8,128)(2,1)}, bf16[512,128]{1,0:T(8,128)(2,1)}) custom-call(bf16[512,128]{1,0:T(8,128)(2,1)} %get-tuple-element.8.refs_0_, bf16[512,128]{1,0:T(8,128)(2,1)} %get-tuple-element.9.refs_1_, bf16[512,128]{1,0:T(8,128)(2,1)} %get-tuple-element.10.refs_2_, ...), custom_call_target="tpu_custom_call" | custom-call | tf_op jit(solution)/shard_map/pallas_call | solution.py:546
  (2 shorter events, 0.0 us)

commit v7 on v5

--- a/solution.py
+++ b/solution.py
@@ -158,6 +158,7 @@
     me.wait(partners)
 
     w_z = [wire.send(w, wcol.at[me.z], me.at_z(j)) for j in range(1, Z)]
+    w_p = [wire.send(w, wall.at[me.z, me.p], me.at_p(j)) for j in range(1, PN)]
     g_a = [
         wire.send(gcand.at[(me.p + j) % PN], ga.at[me.p], me.at_p(j)) for j in range(1, PN)
     ]
@@ -188,10 +189,13 @@
 
 
     wcol[pl.ds(me.z, 1)] = wv[...][None]
-    for copy in w_z:
-        copy.wait_recv()
+    for j in (1, Z - 1, *range(2, Z - 1)):
+        w_z[j - 1].wait_recv()
+        source = (me.z + Z - j) % Z
+        w_p += [
+            wire.send(wcol.at[source], wall.at[source, me.p], me.at_p(i)) for i in range(1, PN)
+        ]
     wall[:, pl.ds(me.p, 1)] = wcol[...][:, None]
-    w_p = [wire.send(wcol, wall.at[:, me.p], me.at_p(j)) for j in range(1, PN)]
 
     pack(0, 0, lambda b: kblk[b], sb0)
     pack(0, 1, lambda b: vblk[b], sb0)
@@ -217,9 +221,10 @@
     chunk_z = Z // Y
     width = L * HEAD_DIM
     y_sends = []
+    y_order = sorted(range(Y), key=lambda j: -min(j, Y - j))
     for part in range(2):
         rows = gov[part * half : (part + 1) * half]
-        for j in list(range(1, Y)) + [0]:
+        for j in y_order:
             to = (me.y + j) % Y
             weight = wall[pl.ds(to * chunk_z, chunk_z)].reshape(width, HEAD_DIM)
             terms = lax.dot_general(

time: 130 us -> 130 us (level)
  the two profiles are of different devices: /device:TPU:89 before, /device:TPU:85 now
where the time goes in v7:
time: 130 us; the launch traced here: 129 us
  Pallas kernels  126 us (97%)
  local copies, waits for them, and re-layouts  2.29 us (2%)
    pallas_call x1, Pallas kernels, per_device(): pl.pallas_call(functools.partial(kernel, dims), out_shape=(shape((tokens,...  125 us

profile of v7, /device:TPU:85, one launch (start us, length us, event | category | flops | bytes accessed | tf_op | source)
XLA Modules:
  0.0 129.4 jit_solution(1312980072358833979)
XLA Ops:
  0.7 0.8 constant_dynamic-slice_fusion
  1.5 0.6 slice_reduce_fusion.shared
  2.1 0.1 copy.13
  2.2 0.1 reshape.19
  2.3 0.7 pad.4.wanted
  2.9 124.5 %shard_map.93 = (bf16[512,128]{1,0:T(8,128)(2,1)}, bf16[512,128]{1,0:T(8,128)(2,1)}, bf16[512,128]{1,0:T(8,128)(2,1)}, bf16[512,128]{1,0:T(8,128)(2,1)}) custom-call(bf16[512,128]{1,0:T(8,128)(2,1)} %q.1, bf16[8,64,128]{2,1,0:T(8,128)(2,1)} %bitcast.5, bf16[8,64,128]{2,1,0:T(8,128)(2,1)} %bitcast.6, bf16[64,128]{1,0:T(8,128)(2,1)} %w.1, ...), custom_call_target="tpu_custom_call" | custom-call | tf_op jit(solution)/shard_map/pallas_call | solution.py:514
  127.5 1.9 %shard_map.94 = (bf16[512,128]{1,0:T(8,128)(2,1)}, bf16[512,128]{1,0:T(8,128)(2,1)}, bf16[512,128]{1,0:T(8,128)(2,1)}, bf16[512,128]{1,0:T(8,128)(2,1)}) custom-call(bf16[512,128]{1,0:T(8,128)(2,1)} %get-tuple-element.8.refs_0_, bf16[512,128]{1,0:T(8,128)(2,1)} %get-tuple-element.9.refs_1_, bf16[512,128]{1,0:T(8,128)(2,1)} %get-tuple-element.10.refs_2_, ...), custom_call_target="tpu_custom_call" | custom-call | tf_op jit(solution)/shard_map/pallas_call | solution.py:550
  (2 shorter events, 0.0 us)

commit v8 on v5

--- a/solution.py
+++ b/solution.py
@@ -325,40 +325,27 @@
     acc = {}
     total = [jnp.zeros((2 * BLOCK, HEAD_DIM), f32) for _ in range(2)]
 
-    def settle(at):
-        for part in range(2):
-            term = acc.pop((at, part))
-            if at < 0:
-                eout[0, part] = term.astype(bf16)
-            elif at >= blocks:
-                eout[1, part] = term.astype(bf16)
-            else:
-                own[part, at] = term
-
-    fr[entries] = jnp.zeros(fr.shape[1:], bf16)
-    for b in range(blocks):
-        qb, gb_rows = qv[span[b]], gctx[span[b]]
-        probs = probs32[b]
-        keys, values = kcat[b], vcat[b]
-        delta = jnp.sum(
-            gb_rows.astype(f32) * ctx[span[b]].astype(f32), axis=-1, keepdims=True
-        )
-        gscores = (probs * (dot(gb_rows, values, nt) - delta)).astype(bf16)
-        dq[span[b]] = (dot(gscores, keys, nn) * SCALE).astype(bf16)
-        for part, term in (
-            (0, dot(gscores, qb, tn) * SCALE),
-            (1, dot(probs.astype(bf16), gb_rows, tn)),
-        ):
-            for i in range(3):
-                at = (b - 1 + i, part)
-                one = term[i * BLOCK : (i + 1) * BLOCK]
-                acc[at] = acc[at] + one if at in acc else one
-            total[part] = total[part] + term[3 * BLOCK : 5 * BLOCK]
-            for i in range(3):
-                fr[b * 3 + i, part] = term[(5 + i) * BLOCK : (6 + i) * BLOCK].astype(bf16)
-        settle(b - 1)
-    settle(blocks - 1)
-    settle(blocks)
+    def settle(at, part):
+        term = acc.pop((at, part))
+        if at < 0:
+            eout[0, part] = term.astype(bf16)
+        elif at >= blocks:
+            eout[1, part] = term.astype(bf16)
+        else:
+            own[part, at] = term
+
+    def add_terms(b, part, term):
+        for i in range(3):
+            at = (b - 1 + i, part)
+            one = term[i * BLOCK : (i + 1) * BLOCK]
+            acc[at] = acc[at] + one if at in acc else one
+        total[part] = total[part] + term[3 * BLOCK : 5 * BLOCK]
+        for i in range(3):
+            fr[b * 3 + i, part] = term[(5 + i) * BLOCK : (6 + i) * BLOCK].astype(bf16)
+        settle(b - 1, part)
+        if b == blocks - 1:
+            settle(b, part)
+            settle(b + 1, part)
 
     landing = (ar0, ar1, ar2, ar3)
     returned = {}
@@ -373,8 +360,21 @@
             for j in range(1, PN)
         ]
 
+    fr[entries] = jnp.zeros(fr.shape[1:], bf16)
+    for b in range(blocks):
+        add_terms(b, 1, dot(probs32[b].astype(bf16), gctx[span[b]], tn))
+    spread(3, 1)
+    for b in range(blocks):
+        qb, gb_rows = qv[span[b]], gctx[span[b]]
+        keys = kcat[b]
+        delta = jnp.sum(
+            gb_rows.astype(f32) * ctx[span[b]].astype(f32), axis=-1, keepdims=True
+        )
+        gscores = (probs32[b] * (dot(gb_rows, vcat[b], nt) - delta)).astype(bf16)
+        dq[span[b]] = (dot(gscores, keys, nn) * SCALE).astype(bf16)
+        add_terms(b, 0, dot(gscores, qb, tn) * SCALE)
+
     spread(3, 0)
-    spread(3, 1)
     for j in range(2):
         for part in range(2):
             first = (j * 2 + part) * pieces
@@ -402,10 +402,10 @@
             sums.append(dot(selects[at], data, tn).reshape(blocks, 16, HEAD_DIM))
         return jnp.concatenate(sums, axis=1)
 
+    p2[1] = gather_sum(3, 1).astype(bf16)
+    far_down = wire.send(p2.at[1], fp, me.at_z(-1))
     p2[0] = gather_sum(3, 0).astype(bf16)
     far_up = wire.send(p2.at[0], fm, me.at_z(1))
-    p2[1] = gather_sum(3, 1).astype(bf16)
-    far_down = wire.send(p2.at[1], fp, me.at_z(-1))
 
     for copy in s_a:
         copy.wait_recv()

time: 130 us -> 130 us (level)
  the two profiles are of different devices: /device:TPU:89 before, /device:TPU:72 now
where the time goes in v8:
time: 130 us
  Pallas kernels  127 us (98%)
  local copies, waits for them, and re-layouts  2.29 us (2%)
    pallas_call x1, Pallas kernels, per_device(): pl.pallas_call(functools.partial(kernel, dims), out_shape=(shape((tokens,...  125 us

profile of v8, /device:TPU:72, one launch (start us, length us, event | category | flops | bytes accessed | tf_op | source)
XLA Modules:
  0.0 129.6 jit_solution(7537617074067111499)
XLA Ops:
  0.7 0.8 constant_dynamic-slice_fusion
  1.5 0.6 slice_reduce_fusion.shared
  2.1 0.1 copy.13
  2.2 0.1 reshape.19
  2.3 0.7 pad.4.wanted
  2.9 124.7 %shard_map.93 = (bf16[512,128]{1,0:T(8,128)(2,1)}, bf16[512,128]{1,0:T(8,128)(2,1)}, bf16[512,128]{1,0:T(8,128)(2,1)}, bf16[512,128]{1,0:T(8,128)(2,1)}) custom-call(bf16[512,128]{1,0:T(8,128)(2,1)} %q.1, bf16[8,64,128]{2,1,0:T(8,128)(2,1)} %bitcast.5, bf16[8,64,128]{2,1,0:T(8,128)(2,1)} %bitcast.6, bf16[64,128]{1,0:T(8,128)(2,1)} %w.1, ...), custom_call_target="tpu_custom_call" | custom-call | tf_op jit(solution)/shard_map/pallas_call | solution.py:509
  127.7 1.9 %shard_map.94 = (bf16[512,128]{1,0:T(8,128)(2,1)}, bf16[512,128]{1,0:T(8,128)(2,1)}, bf16[512,128]{1,0:T(8,128)(2,1)}, bf16[512,128]{1,0:T(8,128)(2,1)}) custom-call(bf16[512,128]{1,0:T(8,128)(2,1)} %get-tuple-element.8.refs_0_, bf16[512,128]{1,0:T(8,128)(2,1)} %get-tuple-element.9.refs_1_, bf16[512,128]{1,0:T(8,128)(2,1)} %get-tuple-element.10.refs_2_, ...), custom_call_target="tpu_custom_call" | custom-call | tf_op jit(solution)/shard_map/pallas_call | solution.py:545
  (2 shorter events, 0.0 us)
